TPU v7x, 512 devices: a whole 4x8x8 slice. The times are simulated.
512 devices in a mesh: attn: 32 (over y, z_hi), ffn: 16 (over x, z_lo, core).
Axes of the slice: x: 4, y: 8, z: 8 (z_hi: 4, z_lo: 2; z = z_hi * 2 + z_lo), core: 2. Of those that a mesh axis runs over, the one named last changes fastest.
Arguments:
- queries: bfloat16 [128, 64, 128], P('attn'), may hold values from -8 to 8
- new_keys: bfloat16 [128, 8, 128], P('attn'), may hold values from -8 to 8
- token_new_values: bfloat16 [128, 8, 128], P('attn'), may hold values from -6 to 6
- cache_keys: bfloat16 [128, 2048, 8, 128], P('attn', 'ffn'), may hold values from -8 to 8
- stored_cache_values: bfloat16 [128, 2048, 8, 128], P('attn', 'ffn'), may hold values from -6 to 6
- lengths: int32 [128], P('attn'), may hold values from 1 to 2048, 163840 in all
- residual_in: bfloat16 [128, 8192], P('ffn', 'attn'), may hold values from -6 to 6
- out_weight: bfloat16 [8192, 8192], P('ffn', 'attn'), may hold values from -0.0625 to 0.0625
- norm_gain: float32 [8192], P('attn'), may hold values from 0.1 to 1.9
- gate_weight: bfloat16 [8192, 14336], P('attn', 'ffn'), may hold values from -0.0625 to 0.0625
- up_weight: bfloat16 [8192, 14336], P('attn', 'ffn'), may hold values from -0.0625 to 0.0625
- down_weight: bfloat16 [14336, 8192], P('ffn', 'attn'), may hold values from -0.046875 to 0.046875
Outputs:
- attended: bfloat16 [128, 8192], P('attn', 'ffn')
- layer_out: bfloat16 [128, 8192], P('ffn', 'attn')
Inputs may be any that keep to these rules, and one draw needn't show every extreme that they name: lengths[r] positions of row r are valid, from position 0; some row has all 2048.
All inputs are finite; a program needn't handle non-finite values. No bound on the sum of `lengths` on one device may be relied on, other than what follows from the above.
Results may differ from a plain program's by a relative error of at most 0.027.
Values may be sent and summed in bfloat16 or wider, within the bound.
A program may use at most 64 MiB of HBM per device.

v0:
```python
import math

import jax
import jax.numpy as jnp
from jax import lax
from jax.sharding import PartitionSpec as P

D = 8192


def merged(shard, axis, combine):
    everything = jax.tree.map(lambda part: lax.all_gather(part, axis), shard)
    leading = jax.tree.map(lambda part: part[0], everything)

    def turn(k, so_far):
        return combine(so_far, jax.tree.map(lambda part: part[k], everything))

    return lax.fori_loop(1, lax.axis_size(axis), turn, leading)


def combine_partials(first_part, second_part):
    first_max, first_total, first_sum = first_part
    second_max, second_total, second_sum = second_part
    joined_max = jnp.maximum(first_max, second_max)
    first_factor = jnp.exp(first_max - joined_max)
    second_factor = jnp.exp(second_max - joined_max)
    joined_total = first_total * first_factor + second_total * second_factor
    joined_sum = first_sum * first_factor[..., None] + second_sum * second_factor[..., None]
    return (joined_max, joined_total, joined_sum)


def on_device(
    queries,
    new_keys,
    token_new_values,
    cache_keys,
    stored_cache_values,
    lengths,
    residual_in,
    out_weight,
    norm_gain,
    gate_weight,
    up_weight,
    down_weight,
):
    row_count, head_count, head_size = queries.shape
    kv_heads = new_keys.shape[1]
    group_size = head_count // kv_heads
    span_len = cache_keys.shape[1]
    block_heads = head_count // lax.axis_size("ffn")
    scale = 1.0 / math.sqrt(head_size)
    first_position = lax.axis_index("ffn") * span_len
    grouped_heads = queries.reshape(row_count, kv_heads, group_size, head_size)
    scores = (
        jnp.einsum("rkgd,rpkd->rkgp", grouped_heads, cache_keys, preferred_element_type=jnp.float32)
        * scale
    )
    positions = first_position + jnp.arange(span_len, dtype=jnp.int32)
    valid = (positions[None, :] < lengths[:, None])[:, None, None, :]
    scores = jnp.where(valid, scores, -1e30)
    local_max = jnp.max(scores, axis=-1)
    weights = jnp.where(valid, jnp.exp(scores - local_max[..., None]), 0.0).astype(jnp.bfloat16)
    local_total = jnp.sum(weights.astype(jnp.float32), axis=-1)
    local_sum = jnp.einsum(
        "rkgp,rpkd->rkgd", weights, stored_cache_values, preferred_element_type=jnp.float32
    )
    local_max = local_max.reshape(row_count, head_count)
    local_total = local_total.reshape(row_count, head_count)
    local_sum = local_sum.reshape(row_count, head_count, head_size)
    head_start = lax.axis_index("ffn") * block_heads
    every_max, every_total, every_sum = merged(
        (local_max, local_total, local_sum), "ffn", combine_partials
    )
    block_max = lax.dynamic_slice_in_dim(every_max, head_start, block_heads, 1)
    block_total = lax.dynamic_slice_in_dim(every_total, head_start, block_heads, 1)
    block_sum = lax.dynamic_slice_in_dim(every_sum, head_start, block_heads, 1)
    own_queries = lax.dynamic_slice_in_dim(queries, head_start, block_heads, 1).astype(jnp.float32)
    own_keys = lax.dynamic_slice_in_dim(
        jnp.repeat(new_keys, group_size, axis=1), head_start, block_heads, 1
    ).astype(jnp.float32)
    own_values = lax.dynamic_slice_in_dim(
        jnp.repeat(token_new_values, group_size, axis=1), head_start, block_heads, 1
    ).astype(jnp.float32)
    own_score = jnp.sum(own_queries * own_keys, axis=-1) * scale
    highest = jnp.maximum(block_max, own_score)
    cache_factor = jnp.exp(block_max - highest)
    own_weight = jnp.exp(own_score - highest)
    total = block_total * cache_factor + own_weight
    summed = block_sum * cache_factor[..., None] + own_weight[..., None] * own_values
    attended = (
        (summed / total[..., None]).reshape(row_count, block_heads * head_size).astype(jnp.bfloat16)
    )
    terms = jnp.dot(
        lax.all_gather(attended, "attn", axis=0, tiled=True),
        out_weight,
        preferred_element_type=jnp.float32,
    )
    projected = lax.psum_scatter(terms, "ffn", scatter_dimension=0, tiled=True)
    mixed = (residual_in.astype(jnp.float32) + projected).astype(jnp.bfloat16)
    wide = mixed.astype(jnp.float32)
    square_total = lax.psum(jnp.sum(wide * wide, axis=1), "attn")
    normed = (wide * lax.rsqrt(square_total / D + 1e-05)[:, None] * norm_gain[None, :]).astype(
        jnp.bfloat16
    )
    hidden_local = gate_weight.shape[1]
    piece = lax.all_gather(normed, "ffn", axis=0, tiled=True)
    gate_part = jnp.dot(piece, gate_weight, preferred_element_type=jnp.float32)
    up_part = jnp.dot(piece, up_weight, preferred_element_type=jnp.float32)
    partial_sums = jnp.concatenate([gate_part, up_part], axis=1)
    summed_all = lax.psum(partial_sums, "attn")
    hidden = (jax.nn.silu(summed_all[:, :hidden_local]) * summed_all[:, hidden_local:]).astype(
        jnp.bfloat16
    )
    feed = lax.psum_scatter(
        jnp.dot(hidden, down_weight, preferred_element_type=jnp.float32),
        "ffn",
        scatter_dimension=0,
        tiled=True,
    )
    layer_out = (wide + feed).astype(jnp.bfloat16)
    return (attended, layer_out)


def solution(mesh):
    in_specs = (
        P("attn", None, None),
        P("attn", None, None),
        P("attn", None, None),
        P("attn", "ffn", None, None),
        P("attn", "ffn", None, None),
        P("attn"),
        P("ffn", "attn"),
        P("ffn", "attn"),
        P("attn"),
        P("attn", "ffn"),
        P("attn", "ffn"),
        P("ffn", "attn"),
    )
    out_specs = (P("attn", "ffn"), P("ffn", "attn"))
    return jax.shard_map(
        on_device, mesh=mesh, in_specs=in_specs, out_specs=out_specs, check_vma=False
    )
```

profile of v0, /device:TPU:1, one launch (start us, length us, event | category | flops | bytes accessed | tf_op | source)
XLA Modules:
  0.0 695.6 jit_solution(5935663303511257853)
XLA Ops:
  8.4 1.6 fusion.22
  10.0 2.4 convolution_bitcast_fusion
  13.6 22.8 %all_gather.16 = f32[16,4,64]{2,1,0:T(4,128)S(1)} all-gather(f32[1,4,64]{2,1,0:T(4,128)S(1)} %all_gather_reshape.10), channel_id=1, replica_groups=mesh['attn'=32,'ffn'=16] {'ffn'}, dimensions={0}, use_global_device_ids=true | all-gather | bytes 17408 | tf_op jit(solution)/shard_map/all_gather | solution.py:12
  36.4 18.0 %all_gather.15 = f32[16,4,64]{2,1,0:T(4,128)S(1)} all-gather(f32[1,4,64]{2,1,0:T(4,128)S(1)} %all_gather_reshape.9), channel_id=1, replica_groups=mesh['attn'=32,'ffn'=16] {'ffn'}, dimensions={0}, use_global_device_ids=true | all-gather | bytes 17408 | tf_op jit(solution)/shard_map/all_gather | solution.py:12
  54.4 3.4 all-gather.3.cloned.1.call-done
  58.7 16.9 %while.19 = (s32[]{:T(128)}, f32[4,64]{1,0:T(4,128)S(1)}, f32[4,64]{1,0:T(4,128)S(1)}, f32[4,64,128]{2,1,0:T(8,128)S(1)}, f32[16,4,64]{2,1,0:T(4,128)S(1)}, /*in...) while((s32[]{:T(128)}, f32[4,64]{1,0:T(4,128)S(1)}, ...), condition=%wide.region_3.4_spmd, body=%wide.region_2.3_spmd.sunk | while | flops 99845 | bytes 403607 | solution.py:18
  58.8 1.1 fusion.36
  61.0 1.1 fusion.36
  62.2 1.1 fusion.36
  63.3 1.1 fusion.36
  64.4 1.1 fusion.36
  65.5 1.1 fusion.36
  66.6 1.1 fusion.36
  67.8 1.1 fusion.36
  68.9 1.1 fusion.36
  70.0 1.1 fusion.36
  75.8 68.7 %all-gather = bf16[32,4,512]{2,1,0:T(4,128)(2,1)S(1)} all-gather(bf16[1,4,512]{2,1,0:T(4,128)(2,1)S(1)} %reshape.53), channel_id=1, replica_groups=mesh['attn'=32,'ffn'=16] {'attn'}, dimensions={0}, use_global_device_ids=true | all-gather | bytes 135168 | tf_op jit(solution)/shard_map/all_gather | solution.py:94
  145.4 69.0 %reduce-scatter.3.cloned.1.call-done = f32[8,256]{1,0:T(8,128)} async-done(((f32[128,256]{1,0:T(8,128)}), f32[8,256]{1,0:T(8,128)}) %reduce-scatter.3.cloned.1.call-update) | async-done | bytes 8208 | tf_op jit(solution)/shard_map/reduce_scatter | solution.py:98
  215.2 68.8 %psum.14 = f32[8]{0:T(128)S(1)} all-reduce(f32[8]{0:T(128)S(1)} %get-tuple-element.201), channel_id=1, replica_groups=mesh['attn'=32,'ffn'=16] {'attn'}, use_global_device_ids=true, to_apply=%region_7.8 | all-reduce | flops 8 | bytes 64 | tf_op jit(solution)/shard_map/psum | solution.py:101
  284.1 33.4 %all_gather.19 = bf16[128,256]{1,0:T(8,128)(2,1)S(1)} all-gather(bf16[8,256]{1,0:T(8,128)(2,1)S(1)} %fusion.12), channel_id=1, replica_groups=mesh['attn'=32,'ffn'=16] {'ffn'}, dimensions={0}, use_global_device_ids=true | all-gather | bytes 69632 | tf_op jit(solution)/shard_map/all_gather | solution.py:106
  319.0 287.7 %all-reduce.2.cloned.1.call-done = f32[128,1792]{1,0:T(8,128)} async-done(((f32[128,1792]{1,0:T(8,128)}), f32[128,1792]{1,0:T(8,128)}) %all-reduce.2.cloned.1.call-update) | async-done | bytes 917520 | tf_op jit(solution)/shard_map/psum | solution.py:110
  606.8 2.1 fusion.7
  609.5 78.2 %reduce-scatter.5.cloned.1.call-done = f32[8,256]{1,0:T(8,128)} async-done(((f32[128,256]{1,0:T(8,128)}), f32[8,256]{1,0:T(8,128)}) %reduce-scatter.5.cloned.1.call-update) | async-done | bytes 8208 | tf_op jit(solution)/shard_map/reduce_scatter | solution.py:114
  687.7 1.3 fusion.13
  (69 shorter events, 13.3 us)
Async XLA Ops:
  7.2 1.2 copy-start
  7.2 5.6 copy-start.4
  7.2 47.2 %copy-start.5 = (bf16[4,8,128]{2,1,0:T(8,128)(2,1)S(1)}, bf16[4,8,128]{2,1,0:T(8,128)(2,1)}, u32[]{:S(2)}) copy-start(bf16[4,8,128]{2,1,0:T(8,128)(2,1)} %param.16) | copy-start | bytes 24580
  7.2 50.6 %all-gather.3.cloned.1.call-start = ((), (), s32[]{:S(2)}) async-start(), calls=%async_computation.2 | async-start | bytes 2228224 | tf_op jit(solution)/shard_map/all_gather | solution.py:12
  12.3 132.2 %copy-start.3 = (bf16[512,256]{1,0:T(8,128)(2,1)S(1)}, bf16[512,256]{1,0:T(8,128)(2,1)}, u32[]{:S(2)}) copy-start(bf16[512,256]{1,0:T(8,128)(2,1)} %param.21) | copy-start | bytes 786436
  12.3 202.0 %copy-start.6 = (bf16[8,256]{1,0:T(8,128)(2,1)S(1)}, bf16[8,256]{1,0:T(8,128)(2,1)}, u32[]{:S(2)}) copy-start(bf16[8,256]{1,0:T(8,128)(2,1)} %param.20) | copy-start | bytes 12292
  12.4 271.6 %copy-start.7 = (f32[256]{0:T(256)S(1)}, f32[256]{0:T(256)}, u32[]{:S(2)}) copy-start(f32[256]{0:T(256)} %param.22) | copy-start | bytes 3076
  12.4 202.0 %reduce-scatter.3.cloned.1.call-start = ((), (), s32[]{:S(2)}) async-start(), calls=%async_computation.3 | async-start | bytes 139264 | tf_op jit(solution)/shard_map/reduce_scatter | solution.py:98
  12.5 304.9 %copy-start.1 = (bf16[256,896]{1,0:T(8,128)(2,1)S(1)}, bf16[256,896]{1,0:T(8,128)(2,1)}, u32[]{:S(2)}) copy-start(bf16[256,896]{1,0:T(8,128)(2,1)} %param.23) | copy-start | bytes 1376260
  58.7 259.0 %copy-start.2 = (bf16[256,896]{1,0:T(8,128)(2,1)S(1)}, bf16[256,896]{1,0:T(8,128)(2,1)}, u32[]{:S(2)}) copy-start(bf16[256,896]{1,0:T(8,128)(2,1)} %param.24) | copy-start | bytes 1376260
  145.4 461.4 %all-reduce.2.cloned.1.call-start = ((), (), s32[]{:S(2)}) async-start(), calls=%async_computation.4 | async-start | bytes 1835008 | tf_op jit(solution)/shard_map/psum | solution.py:110
  317.7 289.1 %copy-start.8 = (bf16[896,256]{1,0:T(8,128)(2,1)S(1)}, bf16[896,256]{1,0:T(8,128)(2,1)}, u32[]{:S(2)}) copy-start(bf16[896,256]{1,0:T(8,128)(2,1)} %param.25) | copy-start | bytes 1376260
  319.0 368.7 %reduce-scatter.5.cloned.1.call-start = ((), (), s32[]{:S(2)}) async-start(), calls=%async_computation.5 | async-start | bytes 139264 | tf_op jit(solution)/shard_map/reduce_scatter | solution.py:114
Sparse Core Ops, SparseCore 0:
  12.5 45.2 all-gather.2
  145.5 68.8 reduce-scatter.2
  319.1 287.6 all-reduce.1
  609.4 78.2 reduce-scatter.4
where the time goes:
time: 698 us; the launch traced here: 696 us
  waiting for transfers between devices  438 us (63%)
  blocking collectives  212 us (30%)
  other arithmetic  21.7 us (3%)
  between operations  13.9 us (2%)
  matrix products  7.3 us (1%)
    psum x1, waiting for transfers between devices, on_device(): summed_all = lax.psum(partial_sums, 'attn')  288 us
    reduce_scatter x1, waiting for transfers between devices, on_device(): lax.psum_scatter(jnp.dot(hidden, down_weight, preferred_element_type=jnp....  78.2 us
    reduce_scatter x1, waiting for transfers between devices, on_device(): projected = lax.psum_scatter(terms, 'ffn', scatter_dimension=0, tiled=True)  69 us
    psum x1, blocking collectives, on_device(): square_total = lax.psum(jnp.sum(wide * wide, axis=1), 'attn')  68.8 us
    all_gather x1, blocking collectives, on_device(): lax.all_gather(attended, 'attn', axis=0, tiled=True)  68.7 us
    all_gather x2, blocking collectives, merged(): everything = jax.tree.map(lambda part: lax.all_gather(part, axis), shard)  40.8 us
    all_gather x1, blocking collectives, on_device(): piece = lax.all_gather(normed, 'ffn', axis=0, tiled=True)  33.4 us
    add x15, other arithmetic, combine_partials(): first_sum * first_factor[..., None] + second_sum * second_factor[..., None]  16.1 us
  transfers between devices with their start and end apart: 4, of which 4 were waited for; matrix products, arithmetic and copies ran while one was open for 0% of the time, Pallas kernels for 0%

commit v1 on v0

v1 whole, which is shorter than its diff:
```python
import functools
import math

import jax
import jax.numpy as jnp
from jax import lax
from jax.experimental import pallas as pl
from jax.experimental.pallas import tpu as pltpu
from jax.sharding import PartitionSpec as P

MESH = pl.DeviceIdType.MESH
D = 8192
A = 32
F = 16
ROWS = 4
HEADS = 64
KV = 8
HD = 128
SPAN = 128
LOW = -1e30
FLOOR = -1e29
BF = jnp.bfloat16
F32 = jnp.float32


def dot(a, b):
    return jnp.dot(a, b, preferred_element_type=F32)


def dot_nt(a, b):
    return lax.dot_general(a, b, (((1,), (1,)), ((), ())), preferred_element_type=F32)


def kernel(
    q_ref, nk_ref, nv_ref, k_hbm, v_hbm, len_ref, res_ref, wo_hbm, gain_ref, wg_hbm, wu_hbm, wd_hbm,
    att_out, layer_out,
    k_s, v_s, wo_s, wg_s, wu_s, wd_s,
    snd_a, rcv_a, msg_b, rcv_b, snd_c, rcv_c, msg_e, rcv_e, snd_f, rcv_f, msg_g, rcv_g, snd_h, rcv_h,
    x_s, att_s, gath_s,
    load_sem, send_sem, recv_sem, recv_f_sem,
):
    a = lax.axis_index("attn")
    f = lax.axis_index("ffn")

    loads = [
        pltpu.make_async_copy(src, dst, load_sem.at[i])
        for i, (src, dst) in enumerate(
            [(k_hbm, k_s), (v_hbm, v_s), (wo_hbm, wo_s), (wg_hbm, wg_s), (wu_hbm, wu_s), (wd_hbm, wd_s)]
        )
    ]
    for load in loads:
        load.start()

    barrier = pltpu.get_barrier_semaphore()

    def greet_f(i, c):
        pl.semaphore_signal(barrier, inc=1, device_id=(a, lax.rem(f + i, F)), device_id_type=MESH)
        return c

    def greet_a(i, c):
        pl.semaphore_signal(barrier, inc=1, device_id=(lax.rem(a + i, A), f), device_id_type=MESH)
        return c

    lax.fori_loop(1, F, greet_f, 0)
    lax.fori_loop(1, A, greet_a, 0)

    def to_ffn(src_of, dst, phase):
        def body(i, c):
            to = lax.rem(f + i, F)
            pltpu.make_async_remote_copy(
                src_ref=src_of(to), dst_ref=dst.at[f], send_sem=send_sem.at[phase], recv_sem=recv_sem.at[phase],
                device_id=(a, to), device_id_type=MESH,
            ).start()
            return c

        lax.fori_loop(1, F, body, 0)

    def to_attn(src_of, dst, phase, sem_of):
        def body(i, c):
            to = lax.rem(a + i, A)
            pltpu.make_async_remote_copy(
                src_ref=src_of(to), dst_ref=dst.at[a], send_sem=send_sem.at[phase], recv_sem=sem_of,
                device_id=(to, f), device_id_type=MESH,
            ).start()
            return c

        lax.fori_loop(1, A, body, 0)

    def wait_all(buf, n, sem):
        view = buf.at[pl.ds(0, n - 1)]
        pltpu.make_async_copy(view, view, sem).wait()

    col = lax.broadcasted_iota(jnp.int32, (HEADS, SPAN * KV), 1)
    head = lax.broadcasted_iota(jnp.int32, (HEADS, SPAN * KV), 0)
    match = (col & 7) == (head >> 3)
    place = (col >> 3) + f * SPAN
    own_ok = jnp.logical_and(
        match[:, :HD], jnp.logical_and(col[:, :HD] < KV, jnp.full((HEADS, HD), f, jnp.int32) == 0)
    )
    low_lane = lax.broadcasted_iota(jnp.int32, (HEADS, HD), 1) < HD // 2
    scale = 1.0 / math.sqrt(HD)
    pad = jnp.zeros((HD - KV, HD), BF)
    loads[0].wait()
    loads[1].wait()
    for r in range(ROWS):
        q = q_ref[r]
        s = dot_nt(q, k_s[r]) * scale
        s = jnp.where(jnp.logical_and(match, place < len_ref[r]), s, LOW)
        own = dot_nt(q, jnp.concatenate([nk_ref[r], pad], axis=0)) * scale
        own = jnp.where(own_ok, own, LOW)
        m = jnp.maximum(jnp.max(s, axis=1, keepdims=True), jnp.max(own, axis=1, keepdims=True))
        m = jnp.maximum(m, FLOOR).astype(BF).astype(F32)
        p = jnp.exp(s - m).astype(BF)
        own_p = jnp.exp(own - m).astype(BF)
        total = jnp.sum(p.astype(F32), axis=1, keepdims=True) + jnp.sum(
            own_p.astype(F32), axis=1, keepdims=True
        )
        o = dot(p, v_s[r]) + dot(own_p, jnp.concatenate([nv_ref[r], pad], axis=0))
        stats = jnp.where(low_lane, jnp.broadcast_to(m, (HEADS, HD)), jnp.broadcast_to(total, (HEADS, HD)))
        x_s[pl.ds(r * HEADS, HEADS), :] = jnp.concatenate([o, stats], axis=1).astype(BF)
    n = ROWS * HEADS
    i = lax.broadcasted_iota(jnp.int32, (n, n), 0)
    j = lax.broadcasted_iota(jnp.int32, (n, n), 1)
    perm = (j == ((i >> 2) & 3) * HEADS + (i >> 4) * 4 + (i & 3)).astype(F32).astype(BF)
    snd_a[...] = dot(perm, x_s[...]).astype(BF).reshape(F, 16, 2 * HD)

    pl.semaphore_wait(barrier, A + F - 2)
    to_ffn(lambda to: snd_a.at[to], rcv_a, 0)
    rcv_a[f] = snd_a[f]
    wait_all(rcv_a, F, recv_sem.at[0])

    parts = rcv_a[...].astype(F32)
    low3 = lax.broadcasted_iota(jnp.int32, (F, 16, HD), 2) < HD // 2
    stats = parts[:, :, HD:]
    turned = pltpu.roll(stats.reshape(F * 16, HD), HD // 2, 1).reshape(F, 16, HD)
    m = jnp.where(low3, stats, turned)
    t = jnp.where(low3, turned, stats)
    e = jnp.exp(m - jnp.max(m, axis=0, keepdims=True))
    att = jnp.sum(parts[:, :, :HD] * e, axis=0) / jnp.sum(t * e, axis=0)
    msg_b[...] = att.astype(BF)
    to_attn(lambda to: msg_b, rcv_b, 1, recv_sem.at[1])
    rcv_b[a] = msg_b[...]
    att_s[...] = msg_b[...].astype(F32)
    for h in range(4):
        att_out[:, h * HD : (h + 1) * HD] = att_s[pl.ds(h, ROWS, stride=4), :].astype(BF)
    loads[2].wait()
    wait_all(rcv_b, A, recv_sem.at[1])

    gath_s[...] = rcv_b[...].astype(F32).reshape(A * 16, HD)
    lhs = jnp.concatenate([gath_s[pl.ds(h, A * ROWS, stride=4), :].astype(BF) for h in range(4)], axis=1)

    def halves(x):
        x = x.reshape(F, 8, 2 * HD)
        return jnp.concatenate([x[:, :, :HD], x[:, :, HD:]], axis=1)

    snd_c[...] = halves(dot(lhs, wo_s[...])).astype(BF)
    to_ffn(lambda to: snd_c.at[to], rcv_c, 2)
    rcv_c[f] = snd_c[f]
    res = res_ref[...].astype(F32)
    res = jnp.concatenate([res[:, :HD], res[:, HD:]], axis=0)
    wait_all(rcv_c, F, recv_sem.at[2])
    msg_e[...] = (res + jnp.sum(rcv_c[...].astype(F32), axis=0)).astype(BF)

    to_ffn(lambda to: msg_e, rcv_e, 3)
    rcv_e[f] = msg_e[...]
    loads[3].wait()
    loads[4].wait()
    wait_all(rcv_e, F, recv_sem.at[3])
    wide = rcv_e[...].astype(F32)
    left = wide[:, :8].reshape(F * 8, HD)
    right = wide[:, 8:].reshape(F * 8, HD)
    squares = jnp.sum(left * left + right * right, axis=1, keepdims=True)
    squares = jnp.broadcast_to(squares, (F * 8, HD)).reshape(F, 8, HD)
    gain = gain_ref[...]
    normed = jnp.concatenate([left * gain[:, :HD], right * gain[:, HD:]], axis=1).astype(BF)

    low_sub = lax.broadcasted_iota(jnp.int32, (F, 8, HD), 1) < 4
    turned = pltpu.roll(squares, 4, 1)
    for at, w, even_fill, odd_fill in ((0, wg_s, turned, squares), (32, wu_s, squares, turned)):
        y = dot(normed, w[...]).reshape(F, 8, 7 * HD)
        c = [y[:, :, k * HD : (k + 1) * HD] for k in range(7)]
        even = jnp.concatenate([c[0], c[1], c[2], jnp.where(low_sub, c[3], even_fill)], axis=1)
        odd = jnp.concatenate([c[4], c[5], c[6], jnp.where(low_sub, odd_fill, c[3])], axis=1)
        snd_f[:, 0, pl.ds(at, 32), :] = even.astype(BF)
        snd_f[:, 1, pl.ds(at, 32), :] = odd.astype(BF)
    to_attn(lambda to: snd_f.at[to // 2, lax.rem(to, 2)], rcv_f, 4, recv_f_sem.at[a])

    def add(i, acc):
        src = lax.rem(a + A - i, A)
        pltpu.make_async_copy(rcv_f.at[src], rcv_f.at[src], recv_f_sem.at[src]).wait()
        return acc + rcv_f[src].astype(F32)

    acc = lax.fori_loop(1, A, add, snd_f[a // 2, lax.rem(a, 2)].astype(F32))
    low8 = lax.broadcasted_iota(jnp.int32, (8, HD), 0) < 4
    is_even = jnp.full((8, HD), lax.rem(a, 2), jnp.int32) == 0
    x, y = acc[24:32], acc[56:64]
    square_even = jnp.where(low8, pltpu.roll(x, 4, 0), y)
    square_odd = jnp.where(low8, x, pltpu.roll(y, 4, 0))
    norm = lax.rsqrt(jnp.where(is_even, square_even, square_odd) / D + 1e-5)
    norm = jnp.concatenate([norm] * 4, axis=0)
    gate = acc[:32] * norm
    up = acc[32:] * norm
    msg_g[...] = (gate / (1.0 + jnp.exp(-gate)) * up).astype(BF)

    to_attn(lambda to: msg_g, rcv_g, 5, recv_sem.at[5])
    rcv_g[a] = msg_g[...]
    loads[5].wait()
    wait_all(rcv_g, A, recv_sem.at[5])
    hid = rcv_g[...].reshape(F, 2, 32, HD).astype(F32)
    even, odd = hid[:, 0], hid[:, 1]
    mid = jnp.where(low_sub, even[:, 24:32], odd[:, 24:32])
    cols = [even[:, :8], even[:, 8:16], even[:, 16:24], mid, odd[:, :8], odd[:, 8:16], odd[:, 16:24]]
    hidden = jnp.concatenate([c.reshape(F * 8, HD) for c in cols], axis=1).astype(BF)
    snd_h[...] = halves(dot(hidden, wd_s[...])).astype(BF)
    to_ffn(lambda to: snd_h.at[to], rcv_h, 6)
    rcv_h[f] = snd_h[f]
    wait_all(rcv_h, F, recv_sem.at[6])
    done = msg_e[...].astype(F32) + jnp.sum(rcv_h[...].astype(F32), axis=0)
    layer_out[...] = jnp.concatenate([done[:8], done[8:]], axis=1).astype(BF)

    wait_all(rcv_a, F, send_sem.at[0])
    wait_all(rcv_b, A, send_sem.at[1])
    wait_all(rcv_c, F, send_sem.at[2])
    wait_all(rcv_e, F, send_sem.at[3])
    wait_all(rcv_f, A, send_sem.at[4])
    wait_all(rcv_g, A, send_sem.at[5])
    wait_all(rcv_h, F, send_sem.at[6])


def on_device(q, nk, nv, ck, cv, lengths, res, wo, gain, wg, wu, wd):
    vmem = pl.BlockSpec(memory_space=pltpu.VMEM)
    hbm = pl.BlockSpec(memory_space=pl.ANY)
    smem = pl.BlockSpec(memory_space=pltpu.SMEM)
    V = pltpu.VMEM
    return pl.pallas_call(
        kernel,
        out_shape=(
            jax.ShapeDtypeStruct((ROWS, 4 * HD), BF),
            jax.ShapeDtypeStruct((8, 2 * HD), BF),
        ),
        in_specs=[vmem, vmem, vmem, hbm, hbm, smem, vmem, hbm, vmem, hbm, hbm, hbm],
        out_specs=(vmem, vmem),
        scratch_shapes=[
            V((ROWS, SPAN * KV, HD), BF),
            V((ROWS, SPAN * KV, HD), BF),
            V(wo.shape, BF),
            V(wg.shape, BF),
            V(wu.shape, BF),
            V(wd.shape, BF),
            V((F, 16, 2 * HD), BF),
            V((F, 16, 2 * HD), BF),
            V((16, HD), BF),
            V((A, 16, HD), BF),
            V((F, 16, HD), BF),
            V((F, 16, HD), BF),
            V((16, HD), BF),
            V((F, 16, HD), BF),
            V((F, 2, 64, HD), BF),
            V((A, 64, HD), BF),
            V((32, HD), BF),
            V((A, 32, HD), BF),
            V((F, 16, HD), BF),
            V((F, 16, HD), BF),
            V((ROWS * HEADS, 2 * HD), BF),
            V((16, HD), F32),
            V((A * 16, HD), F32),
            pltpu.SemaphoreType.DMA((6,)),
            pltpu.SemaphoreType.DMA((7,)),
            pltpu.SemaphoreType.DMA((7,)),
            pltpu.SemaphoreType.DMA((A,)),
        ],
        compiler_params=pltpu.CompilerParams(
            collective_id=0, has_side_effects=True, vmem_limit_bytes=40 * 1024 * 1024
        ),
    )(
        q, nk, nv,
        ck.reshape(ROWS, SPAN * KV, HD), cv.reshape(ROWS, SPAN * KV, HD),
        lengths, res, wo, gain.reshape(1, 2 * HD), wg, wu, wd,
    )


def solution(mesh):
    in_specs = (
        P("attn", None, None),
        P("attn", None, None),
        P("attn", None, None),
        P("attn", "ffn", None, None),
        P("attn", "ffn", None, None),
        P("attn"),
        P("ffn", "attn"),
        P("ffn", "attn"),
        P("attn"),
        P("attn", "ffn"),
        P("attn", "ffn"),
        P("ffn", "attn"),
    )
    return jax.shard_map(
        on_device, mesh=mesh, in_specs=in_specs, out_specs=(P("attn", "ffn"), P("ffn", "attn")), check_vma=False
    )
```

time: 698 us -> 82.9 us (0.12)
  waiting for transfers between devices: 438 us -> 0 us
  blocking collectives: 212 us -> 0 us
  Pallas kernels: 0 us -> 71.2 us
  other arithmetic: 21.7 us -> 0 us
  between operations: 13.9 us -> 0.68 us
  local copies, waits for them, and re-layouts: 2.14 us -> 10.5 us
  matrix products: 7.3 us -> 0 us
    psum x1 -> x0, waiting for transfers between devices: 288 us -> none  [on_device(): summed_all = lax.psum(partial_sums, 'attn')]
    reduce_scatter x2 -> x0, waiting for transfers between devices: 147 us -> none  [the longest x1 78.2 us: on_device(): lax.psum_scatter(jnp.dot(hidden, down_weight, preferred_element_type=jnp....]
    all_gather x4 -> x0, blocking collectives: 143 us -> none  [the longest x1 68.7 us: on_device(): lax.all_gather(attended, 'attn', axis=0, tiled=True)]
    pallas_call x0 -> x1, Pallas kernels: none -> 71.2 us  [on_device(): pl.pallas_call(kernel, out_shape=(jax.ShapeDtypeStruct((ROWS, 4 * HD), BF...]
    psum x1 -> x0, blocking collectives: 68.8 us -> none  [on_device(): square_total = lax.psum(jnp.sum(wide * wide, axis=1), 'attn')]
    add x32 -> x0, other arithmetic: 16.6 us -> none  [the longest x15 16.1 us: combine_partials(): first_sum * first_factor[..., None] + second_sum * second_factor[..., None]]
    unnamed x21 -> x26, local copies, waits for them, and re-layouts: 1.04 us -> 10.5 us
    dot_general x6 -> x0, matrix products: 7.3 us -> none  [the longest x1 2.36 us: on_device(): jnp.einsum('rkgp,rpkd->rkgd', weights, stored_cache_values, preferred_ele...]
  transfers between devices with their start and end apart: 4 -> 0, of which waited for: 4 -> 0; matrix products, arithmetic and copies ran while one was open for 0% -> 0% of each run, Pallas kernels for 0% -> 0%
where the time goes in v1:
time: 82.9 us; the launch traced here: 82.4 us
  Pallas kernels  71.2 us (86%)
  local copies, waits for them, and re-layouts  10.5 us (13%)
    pallas_call x1, Pallas kernels, on_device(): pl.pallas_call(kernel, out_shape=(jax.ShapeDtypeStruct((ROWS, 4 * HD), BF...  71.2 us
    unnamed x26, local copies, waits for them, and re-layouts  10.5 us

profile of v1, /device:TPU:1, one launch (start us, length us, event | category | flops | bytes accessed | tf_op | source)
XLA Modules:
  0.0 82.4 jit_solution(14565318947249459673)
XLA Ops:
  0.6 0.0 copy-start.9
  0.6 0.0 copy-start.10
  0.7 0.0 copy-start.11
  0.7 0.7 copy-done.9
  1.3 0.0 copy-done.10
  1.3 0.0 copy-done.11
  1.3 0.0 copy-start
  1.3 1.2 %copy-done = bf16[4,128,8,128]{3,2,1,0:T(8,128)(2,1)S(1)} copy-done((bf16[4,128,8,128]{3,2,1,0:T(8,128)(2,1)S(1)}, bf16[4,128,8,128]{3,2,1,0:T(8,128)(2,1)}, u32[]{:S(2)}) %copy-start) | copy-done | bytes 1048600
  2.6 1.2 %copy-done.1 = bf16[4,128,8,128]{3,2,1,0:T(8,128)(2,1)S(1)} copy-done((bf16[4,128,8,128]{3,2,1,0:T(8,128)(2,1)S(1)}, bf16[4,128,8,128]{3,2,1,0:T(8,128)(2,1)}, u32[]{:S(2)}) %copy-start.1) | copy-done | bytes 1048600
  3.8 0.0 copy-start.2
  3.8 1.0 %copy-done.2 = bf16[256,896]{1,0:T(8,128)(2,1)S(1)} copy-done((bf16[256,896]{1,0:T(8,128)(2,1)S(1)}, bf16[256,896]{1,0:T(8,128)(2,1)}, u32[]{:S(2)}) %copy-start.2) | copy-done | bytes 458776
  4.8 0.0 copy-start.3
  4.8 1.0 %copy-done.3 = bf16[256,896]{1,0:T(8,128)(2,1)S(1)} copy-done((bf16[256,896]{1,0:T(8,128)(2,1)S(1)}, bf16[256,896]{1,0:T(8,128)(2,1)}, u32[]{:S(2)}) %copy-start.3) | copy-done | bytes 458776
  5.8 0.0 copy-start.4
  5.8 1.0 %copy-done.4 = bf16[896,256]{1,0:T(8,128)(2,1)S(1)} copy-done((bf16[896,256]{1,0:T(8,128)(2,1)S(1)}, bf16[896,256]{1,0:T(8,128)(2,1)}, u32[]{:S(2)}) %copy-start.4) | copy-done | bytes 458776
  6.8 0.0 copy-start.5
  6.8 0.9 %copy-done.5 = bf16[512,256]{1,0:T(8,128)(2,1)S(1)} copy-done((bf16[512,256]{1,0:T(8,128)(2,1)S(1)}, bf16[512,256]{1,0:T(8,128)(2,1)}, u32[]{:S(2)}) %copy-start.5) | copy-done | bytes 262168
  7.8 0.0 copy-start.6
  7.8 0.8 %copy-done.6 = bf16[4,64,128]{2,1,0:T(8,128)(2,1)S(1)} copy-done((bf16[4,64,128]{2,1,0:T(8,128)(2,1)S(1)}, bf16[4,64,128]{2,1,0:T(8,128)(2,1)}, u32[]{:S(2)}) %copy-start.6) | copy-done | bytes 65560
  8.6 0.7 copy-done.7
  9.3 0.7 copy-done.8
  10.0 71.2 %shard_map.131 = (bf16[4,512]{1,0:T(4,128)(2,1)S(1)}, bf16[8,256]{1,0:T(8,128)(2,1)S(1)}) custom-call(bf16[4,64,128]{2,1,0:T(8,128)(2,1)S(1)} %copy-done.6, bf16[4,8,128]{2,1,0:T(8,128)(2,1)S(1)} %copy-done.7, bf16[4,8,128]{2,1,0:T(8,128)(2,1)S(1)} %copy-done.8, bf16[4,1024,128]{2,1,0:T(8,128)(2,1)S(1)} %bitcast.3, bf16[4,1024,128]{2,1,0:T(8,128)(2,1)S(1)} %bitcast.4, ...), custom_call_target="tpu_custom_call" | custom-call | tf_op jit(solution)/shard_map/pallas_call | solution.py:235
  81.2 0.6 copy.16
  81.8 0.6 copy.17
  (3 shorter events, 0.0 us)
Async XLA Ops:
  0.6 0.7 copy-start.9
  0.6 0.7 copy-start.10
  0.7 0.7 copy-start.11
  1.3 1.2 %copy-start = (bf16[4,128,8,128]{3,2,1,0:T(8,128)(2,1)S(1)}, bf16[4,128,8,128]{3,2,1,0:T(8,128)(2,1)}, u32[]{:S(2)}) copy-start(bf16[4,128,8,128]{3,2,1,0:T(8,128)(2,1)} %param.15) | copy-start | bytes 3145732
  2.6 1.2 %copy-start.1 = (bf16[4,128,8,128]{3,2,1,0:T(8,128)(2,1)S(1)}, bf16[4,128,8,128]{3,2,1,0:T(8,128)(2,1)}, u32[]{:S(2)}) copy-start(bf16[4,128,8,128]{3,2,1,0:T(8,128)(2,1)} %param.16) | copy-start | bytes 3145732
  3.8 1.0 %copy-start.2 = (bf16[256,896]{1,0:T(8,128)(2,1)S(1)}, bf16[256,896]{1,0:T(8,128)(2,1)}, u32[]{:S(2)}) copy-start(bf16[256,896]{1,0:T(8,128)(2,1)} %wg_hbm.1) | copy-start | bytes 1376260
  4.8 1.0 %copy-start.3 = (bf16[256,896]{1,0:T(8,128)(2,1)S(1)}, bf16[256,896]{1,0:T(8,128)(2,1)}, u32[]{:S(2)}) copy-start(bf16[256,896]{1,0:T(8,128)(2,1)} %wu_hbm.1) | copy-start | bytes 1376260
  5.8 1.0 %copy-start.4 = (bf16[896,256]{1,0:T(8,128)(2,1)S(1)}, bf16[896,256]{1,0:T(8,128)(2,1)}, u32[]{:S(2)}) copy-start(bf16[896,256]{1,0:T(8,128)(2,1)} %wd_hbm.1) | copy-start | bytes 1376260
  6.8 0.9 %copy-start.5 = (bf16[512,256]{1,0:T(8,128)(2,1)S(1)}, bf16[512,256]{1,0:T(8,128)(2,1)}, u32[]{:S(2)}) copy-start(bf16[512,256]{1,0:T(8,128)(2,1)} %wo_hbm.1) | copy-start | bytes 786436
  7.8 0.8 %copy-start.6 = (bf16[4,64,128]{2,1,0:T(8,128)(2,1)S(1)}, bf16[4,64,128]{2,1,0:T(8,128)(2,1)}, u32[]{:S(2)}) copy-start(bf16[4,64,128]{2,1,0:T(8,128)(2,1)} %q_ref.1) | copy-start | bytes 196612
  8.6 0.7 copy-start.7
  9.3 0.7 copy-start.8

commit v2 on v1

--- a/solution.py
+++ b/solution.py
@@ -21,6 +21,22 @@
 FLOOR = -1e29
 BF = jnp.bfloat16
 F32 = jnp.float32
+ATTN_SHIFTS = sorted(
+    ((y, z) for y in range(8) for z in range(4) if y or z),
+    key=lambda s: (-(min(s[0], 8 - s[0]) + 2 * min(s[1], 4 - s[1])), s),
+)
+FFN_SHIFTS = sorted(
+    ((x, z, c) for x in range(4) for z in range(2) for c in range(2) if x or z or c),
+    key=lambda s: (-(min(s[0], 4 - s[0]) + s[1] + s[2] / 2), s),
+)
+
+
+def attn_at(a, shift, sign=1):
+    return ((((a >> 2) + sign * shift[0]) & 7) << 2) | ((a + sign * shift[1]) & 3)
+
+
+def ffn_at(f, shift):
+    return ((((f >> 2) + shift[0]) & 3) << 2) | ((f & 3) ^ (2 * shift[1] + shift[2]))
 
 
 def dot(a, b):
@@ -42,14 +58,17 @@
     a = lax.axis_index("attn")
     f = lax.axis_index("ffn")
 
+    def load(src, dst, i):
+        return pltpu.make_async_copy(src, dst, load_sem.at[i])
+
+    caches = [(load(k_hbm.at[r], k_s.at[r], 2 * r), load(v_hbm.at[r], v_s.at[r], 2 * r + 1)) for r in range(ROWS)]
     loads = [
-        pltpu.make_async_copy(src, dst, load_sem.at[i])
-        for i, (src, dst) in enumerate(
-            [(k_hbm, k_s), (v_hbm, v_s), (wo_hbm, wo_s), (wg_hbm, wg_s), (wu_hbm, wu_s), (wd_hbm, wd_s)]
-        )
+        load(src, dst, 2 * ROWS + i)
+        for i, (src, dst) in enumerate([(wo_hbm, wo_s), (wg_hbm, wg_s), (wu_hbm, wu_s), (wd_hbm, wd_s)])
     ]
-    for load in loads:
-        load.start()
+    for pair in caches:
+        for copy in pair:
+            copy.start()
 
     barrier = pltpu.get_barrier_semaphore()
 
@@ -65,26 +84,20 @@
     lax.fori_loop(1, A, greet_a, 0)
 
     def to_ffn(src_of, dst, phase):
-        def body(i, c):
-            to = lax.rem(f + i, F)
+        for shift in FFN_SHIFTS:
+            to = ffn_at(f, shift)
             pltpu.make_async_remote_copy(
                 src_ref=src_of(to), dst_ref=dst.at[f], send_sem=send_sem.at[phase], recv_sem=recv_sem.at[phase],
                 device_id=(a, to), device_id_type=MESH,
             ).start()
-            return c
-
-        lax.fori_loop(1, F, body, 0)
 
     def to_attn(src_of, dst, phase, sem_of):
-        def body(i, c):
-            to = lax.rem(a + i, A)
+        for shift in ATTN_SHIFTS:
+            to = attn_at(a, shift)
             pltpu.make_async_remote_copy(
                 src_ref=src_of(to), dst_ref=dst.at[a], send_sem=send_sem.at[phase], recv_sem=sem_of,
                 device_id=(to, f), device_id_type=MESH,
             ).start()
-            return c
-
-        lax.fori_loop(1, A, body, 0)
 
     def wait_all(buf, n, sem):
         view = buf.at[pl.ds(0, n - 1)]
@@ -100,10 +113,9 @@
     low_lane = lax.broadcasted_iota(jnp.int32, (HEADS, HD), 1) < HD // 2
     scale = 1.0 / math.sqrt(HD)
     pad = jnp.zeros((HD - KV, HD), BF)
-    loads[0].wait()
-    loads[1].wait()
     for r in range(ROWS):
         q = q_ref[r]
+        caches[r][0].wait()
         s = dot_nt(q, k_s[r]) * scale
         s = jnp.where(jnp.logical_and(match, place < len_ref[r]), s, LOW)
         own = dot_nt(q, jnp.concatenate([nk_ref[r], pad], axis=0)) * scale
@@ -115,9 +127,12 @@
         total = jnp.sum(p.astype(F32), axis=1, keepdims=True) + jnp.sum(
             own_p.astype(F32), axis=1, keepdims=True
         )
+        caches[r][1].wait()
         o = dot(p, v_s[r]) + dot(own_p, jnp.concatenate([nv_ref[r], pad], axis=0))
         stats = jnp.where(low_lane, jnp.broadcast_to(m, (HEADS, HD)), jnp.broadcast_to(total, (HEADS, HD)))
         x_s[pl.ds(r * HEADS, HEADS), :] = jnp.concatenate([o, stats], axis=1).astype(BF)
+    for copy in loads:
+        copy.start()
     n = ROWS * HEADS
     i = lax.broadcasted_iota(jnp.int32, (n, n), 0)
     j = lax.broadcasted_iota(jnp.int32, (n, n), 1)
@@ -143,7 +158,7 @@
     att_s[...] = msg_b[...].astype(F32)
     for h in range(4):
         att_out[:, h * HD : (h + 1) * HD] = att_s[pl.ds(h, ROWS, stride=4), :].astype(BF)
-    loads[2].wait()
+    loads[0].wait()
     wait_all(rcv_b, A, recv_sem.at[1])
 
     gath_s[...] = rcv_b[...].astype(F32).reshape(A * 16, HD)
@@ -163,8 +178,8 @@
 
     to_ffn(lambda to: msg_e, rcv_e, 3)
     rcv_e[f] = msg_e[...]
-    loads[3].wait()
-    loads[4].wait()
+    loads[1].wait()
+    loads[2].wait()
     wait_all(rcv_e, F, recv_sem.at[3])
     wide = rcv_e[...].astype(F32)
     left = wide[:, :8].reshape(F * 8, HD)
@@ -185,12 +200,11 @@
         snd_f[:, 1, pl.ds(at, 32), :] = odd.astype(BF)
     to_attn(lambda to: snd_f.at[to // 2, lax.rem(to, 2)], rcv_f, 4, recv_f_sem.at[a])
 
-    def add(i, acc):
-        src = lax.rem(a + A - i, A)
+    acc = snd_f[a // 2, lax.rem(a, 2)].astype(F32)
+    for shift in reversed(ATTN_SHIFTS):
+        src = attn_at(a, shift, -1)
         pltpu.make_async_copy(rcv_f.at[src], rcv_f.at[src], recv_f_sem.at[src]).wait()
-        return acc + rcv_f[src].astype(F32)
-
-    acc = lax.fori_loop(1, A, add, snd_f[a // 2, lax.rem(a, 2)].astype(F32))
+        acc = acc + rcv_f[src].astype(F32)
     low8 = lax.broadcasted_iota(jnp.int32, (8, HD), 0) < 4
     is_even = jnp.full((8, HD), lax.rem(a, 2), jnp.int32) == 0
     x, y = acc[24:32], acc[56:64]
@@ -204,7 +218,7 @@
 
     to_attn(lambda to: msg_g, rcv_g, 5, recv_sem.at[5])
     rcv_g[a] = msg_g[...]
-    loads[5].wait()
+    loads[3].wait()
     wait_all(rcv_g, A, recv_sem.at[5])
     hid = rcv_g[...].reshape(F, 2, 32, HD).astype(F32)
     even, odd = hid[:, 0], hid[:, 1]
@@ -264,13 +278,13 @@
             V((ROWS * HEADS, 2 * HD), BF),
             V((16, HD), F32),
             V((A * 16, HD), F32),
-            pltpu.SemaphoreType.DMA((6,)),
+            pltpu.SemaphoreType.DMA((2 * ROWS + 4,)),
             pltpu.SemaphoreType.DMA((7,)),
             pltpu.SemaphoreType.DMA((7,)),
             pltpu.SemaphoreType.DMA((A,)),
         ],
         compiler_params=pltpu.CompilerParams(
-            collective_id=0, has_side_effects=True, vmem_limit_bytes=40 * 1024 * 1024
+            collective_id=0, has_side_effects=True, vmem_limit_bytes=60 * 1024 * 1024
         ),
     )(
         q, nk, nv,

time: 82.9 us -> 69.3 us (0.84)
  local copies, waits for them, and re-layouts: 10.5 us -> 1.86 us
  Pallas kernels: 71.2 us -> 66.6 us
    unnamed x26 -> x4, local copies, waits for them, and re-layouts: 10.5 us -> 1.86 us
    pallas_call x1, Pallas kernels: 71.2 us -> 66.6 us  [on_device(): pl.pallas_call(kernel, out_shape=(jax.ShapeDtypeStruct((ROWS, 4 * HD), BF...]
where the time goes in v2:
time: 69.3 us; the launch traced here: 69.1 us
  Pallas kernels  66.6 us (96%)
  local copies, waits for them, and re-layouts  1.86 us (3%)
    pallas_call x1, Pallas kernels, on_device(): pl.pallas_call(kernel, out_shape=(jax.ShapeDtypeStruct((ROWS, 4 * HD), BF...  66.6 us
    unnamed x4, local copies, waits for them, and re-layouts  1.86 us

profile of v2, /device:TPU:1, one launch (start us, length us, event | category | flops | bytes accessed | tf_op | source)
XLA Modules:
  0.0 69.1 jit_solution(15087352246860732024)
XLA Ops:
  0.6 66.6 %shard_map.131 = (bf16[4,512]{1,0:T(4,128)(2,1)}, bf16[8,256]{1,0:T(8,128)(2,1)}) custom-call(bf16[4,64,128]{2,1,0:T(8,128)(2,1)} %q_ref.1, bf16[4,8,128]{2,1,0:T(8,128)(2,1)} %nk_ref.1, bf16[4,8,128]{2,1,0:T(8,128)(2,1)} %nv_ref.1, bf16[4,1024,128]{2,1,0:T(8,128)(2,1)} %bitcast.3, bf16[4,1024,128]{2,1,0:T(8,128)(2,1)} %bitcast.4, s32[4]{0:T(128)} %len_ref.1, ...), custom_call_target="tpu_custom_call" | custom-call | tf_op jit(solution)/shard_map/pallas_call | solution.py:249
  67.2 0.0 copy-start
  67.2 1.3 %copy.16 = bf16[4,512]{1,0:T(4,128)(2,1)} copy(bf16[4,512]{1,0:T(4,128)(2,1)} %get-tuple-element.4) | data formatting | bytes 8192
  68.5 0.0 copy-done
  68.5 0.6 copy.17
Async XLA Ops:
  67.2 1.3 %copy-start = (bf16[8,256]{1,0:T(8,128)(2,1)S(1)}, bf16[8,256]{1,0:T(8,128)(2,1)}, u32[]{:S(2)}) copy-start(bf16[8,256]{1,0:T(8,128)(2,1)} %get-tuple-element.5) | copy-start | bytes 12292

commit v3 on v2

--- a/solution.py
+++ b/solution.py
@@ -29,6 +29,11 @@
     ((x, z, c) for x in range(4) for z in range(2) for c in range(2) if x or z or c),
     key=lambda s: (-(min(s[0], 4 - s[0]) + s[1] + s[2] / 2), s),
 )
+COLUMN_SHIFTS = [s for s in ATTN_SHIFTS if s[0] % 2 == 0]
+BLOCK_SHIFTS = sorted(
+    ((x, z, c, w) for x in range(4) for z in range(2) for c in range(2) for w in range(3) if x or z or c or w),
+    key=lambda s: (-(min(s[0], 4 - s[0]) + s[1] + s[2] / 2 + min(s[3], 1)), s),
+)
 
 
 def attn_at(a, shift, sign=1):
@@ -48,40 +53,63 @@
 
 
 def kernel(
-    q_ref, nk_ref, nv_ref, k_hbm, v_hbm, len_ref, res_ref, wo_hbm, gain_ref, wg_hbm, wu_hbm, wd_hbm,
+    q_hbm, nk_hbm, nv_hbm, k_hbm, v_hbm, len_hbm, res_hbm, wo_hbm, gain_hbm, wg_hbm, wu_hbm, wd_hbm,
     att_out, layer_out,
-    k_s, v_s, wo_s, wg_s, wu_s, wd_s,
+    q_ref, nk_ref, nv_ref, len_ref, res_ref, gain_ref, k_s, v_s, wo_s, wg_s, wu_s, wd_s,
     snd_a, rcv_a, msg_b, rcv_b, snd_c, rcv_c, msg_e, rcv_e, snd_f, rcv_f, msg_g, rcv_g, snd_h, rcv_h,
     x_s, att_s, gath_s,
-    load_sem, send_sem, recv_sem, recv_f_sem,
+    load_sem, send_sem, recv_sem, recv_f_sem, give_send, give_recv,
 ):
     a = lax.axis_index("attn")
     f = lax.axis_index("ffn")
+    odd = (a >> 2) & 1
+    gate_with = a ^ 4
+    up_with = ((((a >> 2) + 2 * odd - 1) & 7) << 2) | (a & 3)
+    owners = (a, gate_with, up_with)
+    group = ((a >> 3) << 2) | (a & 3)
+
+    barrier = pltpu.get_barrier_semaphore()
+    for shift in ATTN_SHIFTS:
+        pl.semaphore_signal(barrier, inc=1, device_id=(attn_at(a, shift), f), device_id_type=MESH)
+    for shift in BLOCK_SHIFTS:
+        if shift[:3] != (0, 0, 0):
+            peer = (owners[shift[3]], ffn_at(f, shift))
+            pl.semaphore_signal(barrier, inc=1, device_id=peer, device_id_type=MESH)
 
     def load(src, dst, i):
         return pltpu.make_async_copy(src, dst, load_sem.at[i])
 
+    small = [
+        load(src, dst, 2 * ROWS + 6 + i)
+        for i, (src, dst) in enumerate(
+            [(q_hbm, q_ref), (nk_hbm, nk_ref), (nv_hbm, nv_ref), (len_hbm, len_ref), (res_hbm, res_ref), (gain_hbm, gain_ref.at[0])]
+        )
+    ]
     caches = [(load(k_hbm.at[r], k_s.at[r], 2 * r), load(v_hbm.at[r], v_s.at[r], 2 * r + 1)) for r in range(ROWS)]
+    own_half = pl.ds(pl.multiple_of(odd * 4 * HD, HD), 3 * HD)
+    their_half = pl.ds(pl.multiple_of((1 - odd) * 4 * HD, HD), 3 * HD)
+    shared = pl.ds(3 * HD, HD)
+    n0 = 2 * ROWS
     loads = [
-        load(src, dst, 2 * ROWS + i)
-        for i, (src, dst) in enumerate([(wo_hbm, wo_s), (wg_hbm, wg_s), (wu_hbm, wu_s), (wd_hbm, wd_s)])
+        load(wo_hbm, wo_s, n0),
+        load(wd_hbm, wd_s, n0 + 1),
+        load(wg_hbm.at[:, own_half], wg_s.at[0, :, pl.ds(0, 3 * HD)], n0 + 2),
+        load(wg_hbm.at[:, shared], wg_s.at[0, :, shared], n0 + 3),
+        load(wu_hbm.at[:, own_half], wu_s.at[0, :, pl.ds(0, 3 * HD)], n0 + 4),
+        load(wu_hbm.at[:, shared], wu_s.at[0, :, shared], n0 + 5),
     ]
+
+    def give(src, dst, to, i):
+        return pltpu.make_async_remote_copy(
+            src_ref=src, dst_ref=dst, send_sem=give_send.at[i], recv_sem=give_recv.at[i],
+            device_id=(to, f), device_id_type=MESH,
+        )
+
+    for copy in small:
+        copy.start()
     for pair in caches:
         for copy in pair:
             copy.start()
-
-    barrier = pltpu.get_barrier_semaphore()
-
-    def greet_f(i, c):
-        pl.semaphore_signal(barrier, inc=1, device_id=(a, lax.rem(f + i, F)), device_id_type=MESH)
-        return c
-
-    def greet_a(i, c):
-        pl.semaphore_signal(barrier, inc=1, device_id=(lax.rem(a + i, A), f), device_id_type=MESH)
-        return c
-
-    lax.fori_loop(1, F, greet_f, 0)
-    lax.fori_loop(1, A, greet_a, 0)
 
     def to_ffn(src_of, dst, phase):
         for shift in FFN_SHIFTS:
@@ -113,6 +141,8 @@
     low_lane = lax.broadcasted_iota(jnp.int32, (HEADS, HD), 1) < HD // 2
     scale = 1.0 / math.sqrt(HD)
     pad = jnp.zeros((HD - KV, HD), BF)
+    for copy in small:
+        copy.wait()
     for r in range(ROWS):
         q = q_ref[r]
         caches[r][0].wait()
@@ -139,8 +169,16 @@
     perm = (j == ((i >> 2) & 3) * HEADS + (i >> 4) * 4 + (i & 3)).astype(F32).astype(BF)
     snd_a[...] = dot(perm, x_s[...]).astype(BF).reshape(F, 16, 2 * HD)
 
-    pl.semaphore_wait(barrier, A + F - 2)
+    pl.semaphore_wait(barrier, A - 1 + 3 * (F - 1))
     to_ffn(lambda to: snd_a.at[to], rcv_a, 0)
+    gifts = [
+        give(wg_hbm.at[:, their_half], wg_s.at[1, :, pl.ds(0, 3 * HD)], gate_with, 0),
+        give(wu_hbm.at[:, their_half], wu_s.at[1, :, pl.ds(0, 3 * HD)], up_with, 1),
+        give(wg_hbm.at[:, shared], wg_s.at[1, :, shared], gate_with, 2),
+        give(wu_hbm.at[:, shared], wu_s.at[1, :, shared], up_with, 3),
+        give(gain_ref.at[0], gain_ref.at[1], gate_with, 4),
+        give(gain_ref.at[0], gain_ref.at[2], up_with, 5),
+    ]
     rcv_a[f] = snd_a[f]
     wait_all(rcv_a, F, recv_sem.at[0])
 
@@ -154,6 +192,8 @@
     att = jnp.sum(parts[:, :, :HD] * e, axis=0) / jnp.sum(t * e, axis=0)
     msg_b[...] = att.astype(BF)
     to_attn(lambda to: msg_b, rcv_b, 1, recv_sem.at[1])
+    for gift in gifts:
+        gift.start()
     rcv_b[a] = msg_b[...]
     att_s[...] = msg_b[...].astype(F32)
     for h in range(4):
@@ -176,54 +216,72 @@
     wait_all(rcv_c, F, recv_sem.at[2])
     msg_e[...] = (res + jnp.sum(rcv_c[...].astype(F32), axis=0)).astype(BF)
 
-    to_ffn(lambda to: msg_e, rcv_e, 3)
+    for shift in BLOCK_SHIFTS:
+        pltpu.make_async_remote_copy(
+            src_ref=msg_e, dst_ref=rcv_e.at[shift[3] * F + f], send_sem=send_sem.at[3], recv_sem=recv_sem.at[3],
+            device_id=(owners[shift[3]], ffn_at(f, shift)), device_id_type=MESH,
+        ).start()
     rcv_e[f] = msg_e[...]
-    loads[1].wait()
-    loads[2].wait()
-    wait_all(rcv_e, F, recv_sem.at[3])
-    wide = rcv_e[...].astype(F32)
-    left = wide[:, :8].reshape(F * 8, HD)
-    right = wide[:, 8:].reshape(F * 8, HD)
-    squares = jnp.sum(left * left + right * right, axis=1, keepdims=True)
-    squares = jnp.broadcast_to(squares, (F * 8, HD)).reshape(F, 8, HD)
-    gain = gain_ref[...]
-    normed = jnp.concatenate([left * gain[:, :HD], right * gain[:, HD:]], axis=1).astype(BF)
-
-    low_sub = lax.broadcasted_iota(jnp.int32, (F, 8, HD), 1) < 4
-    turned = pltpu.roll(squares, 4, 1)
-    for at, w, even_fill, odd_fill in ((0, wg_s, turned, squares), (32, wu_s, squares, turned)):
-        y = dot(normed, w[...]).reshape(F, 8, 7 * HD)
-        c = [y[:, :, k * HD : (k + 1) * HD] for k in range(7)]
-        even = jnp.concatenate([c[0], c[1], c[2], jnp.where(low_sub, c[3], even_fill)], axis=1)
-        odd = jnp.concatenate([c[4], c[5], c[6], jnp.where(low_sub, odd_fill, c[3])], axis=1)
-        snd_f[:, 0, pl.ds(at, 32), :] = even.astype(BF)
-        snd_f[:, 1, pl.ds(at, 32), :] = odd.astype(BF)
-    to_attn(lambda to: snd_f.at[to // 2, lax.rem(to, 2)], rcv_f, 4, recv_f_sem.at[a])
-
-    acc = snd_f[a // 2, lax.rem(a, 2)].astype(F32)
-    for shift in reversed(ATTN_SHIFTS):
+    for copy in loads[2:]:
+        copy.wait()
+    for gift in gifts:
+        gift.wait_recv()
+    wait_all(rcv_e, 3 * F, recv_sem.at[3])
+    wide = rcv_e[...].astype(F32).reshape(3, F, 16, HD)
+    squares = jnp.zeros((F * 8, 1), F32)
+    normed = []
+    for w in range(3):
+        left = wide[w, :, :8].reshape(F * 8, HD)
+        right = wide[w, :, 8:].reshape(F * 8, HD)
+        if w < 2:
+            squares = squares + jnp.sum(left * left + right * right, axis=1, keepdims=True)
+        gain = gain_ref[w]
+        normed.append(jnp.concatenate([left * gain[:, :HD], right * gain[:, HD:]], axis=1).astype(BF))
+    squares = jnp.broadcast_to(squares, (F * 8, HD))
+
+    gate = dot(normed[0], wg_s[0]) + dot(normed[1], wg_s[1])
+    up = dot(normed[0], wu_s[0]) + dot(normed[2], wu_s[1])
+    low = lax.broadcasted_iota(jnp.int32, (F * 8, HD), 1) < HD // 2
+    is_odd = jnp.full((F * 8, HD), odd, jnp.int32) == 1
+    gate3, up3 = gate[:, 3 * HD :], up[:, 3 * HD :]
+    gate3 = jnp.where(is_odd, pltpu.roll(gate3, HD // 2, 1), gate3)
+    up3 = jnp.where(is_odd, up3, pltpu.roll(up3, HD // 2, 1))
+    tiles = [gate[:, k * HD : (k + 1) * HD] for k in range(3)] + [jnp.where(low, gate3, up3)]
+    tiles += [up[:, k * HD : (k + 1) * HD] for k in range(3)] + [squares]
+    snd_f[...] = jnp.concatenate([t.reshape(F, 8, HD) for t in tiles], axis=1).astype(BF)
+    for shift in COLUMN_SHIFTS:
+        to = attn_at(a, shift)
+        pltpu.make_async_remote_copy(
+            src_ref=snd_f.at[((to >> 3) << 2) | (to & 3)], dst_ref=rcv_f.at[group], send_sem=send_sem.at[4],
+            recv_sem=recv_f_sem.at[group], device_id=(to, f), device_id_type=MESH,
+        ).start()
+    acc = snd_f[group].astype(F32)
+    for shift in reversed(COLUMN_SHIFTS):
         src = attn_at(a, shift, -1)
+        src = ((src >> 3) << 2) | (src & 3)
         pltpu.make_async_copy(rcv_f.at[src], rcv_f.at[src], recv_f_sem.at[src]).wait()
         acc = acc + rcv_f[src].astype(F32)
-    low8 = lax.broadcasted_iota(jnp.int32, (8, HD), 0) < 4
-    is_even = jnp.full((8, HD), lax.rem(a, 2), jnp.int32) == 0
-    x, y = acc[24:32], acc[56:64]
-    square_even = jnp.where(low8, pltpu.roll(x, 4, 0), y)
-    square_odd = jnp.where(low8, x, pltpu.roll(y, 4, 0))
-    norm = lax.rsqrt(jnp.where(is_even, square_even, square_odd) / D + 1e-5)
+    norm = lax.rsqrt(acc[56:] / D + 1e-5)
     norm = jnp.concatenate([norm] * 4, axis=0)
     gate = acc[:32] * norm
-    up = acc[32:] * norm
-    msg_g[...] = (gate / (1.0 + jnp.exp(-gate)) * up).astype(BF)
+    half = pltpu.roll(gate[24:], HD // 2, 1)
+    up = jnp.concatenate([acc[32:56] * norm[:24], half], axis=0)
+    hidden = gate / (1.0 + jnp.exp(-gate)) * up
+    low = lax.broadcasted_iota(jnp.int32, (8, HD), 1) < HD // 2
+    is_odd = jnp.full((8, HD), odd, jnp.int32) == 1
+    half = jnp.where(is_odd, pltpu.roll(hidden[24:], HD // 2, 1), hidden[24:])
+    msg_g[...] = jnp.concatenate([hidden[:24], half], axis=0).astype(BF)
 
     to_attn(lambda to: msg_g, rcv_g, 5, recv_sem.at[5])
     rcv_g[a] = msg_g[...]
-    loads[3].wait()
+    loads[1].wait()
     wait_all(rcv_g, A, recv_sem.at[5])
-    hid = rcv_g[...].reshape(F, 2, 32, HD).astype(F32)
-    even, odd = hid[:, 0], hid[:, 1]
-    mid = jnp.where(low_sub, even[:, 24:32], odd[:, 24:32])
-    cols = [even[:, :8], even[:, 8:16], even[:, 16:24], mid, odd[:, :8], odd[:, 8:16], odd[:, 16:24]]
+    hid = rcv_g[...].reshape(4, 2, 4, 32, HD).astype(F32)
+    even = hid[:, 0].reshape(F, 32, HD)
+    odds = hid[:, 1].reshape(F, 32, HD)
+    low = lax.broadcasted_iota(jnp.int32, (F, 8, HD), 2) < HD // 2
+    mid = jnp.where(low, even[:, 24:], odds[:, 24:])
+    cols = [even[:, :8], even[:, 8:16], even[:, 16:24], mid, odds[:, :8], odds[:, 8:16], odds[:, 16:24]]
     hidden = jnp.concatenate([c.reshape(F * 8, HD) for c in cols], axis=1).astype(BF)
     snd_h[...] = halves(dot(hidden, wd_s[...])).astype(BF)
     to_ffn(lambda to: snd_h.at[to], rcv_h, 6)
@@ -235,16 +293,17 @@
     wait_all(rcv_a, F, send_sem.at[0])
     wait_all(rcv_b, A, send_sem.at[1])
     wait_all(rcv_c, F, send_sem.at[2])
-    wait_all(rcv_e, F, send_sem.at[3])
-    wait_all(rcv_f, A, send_sem.at[4])
+    wait_all(rcv_e, 3 * F, send_sem.at[3])
+    wait_all(rcv_f, F, send_sem.at[4])
     wait_all(rcv_g, A, send_sem.at[5])
     wait_all(rcv_h, F, send_sem.at[6])
+    for gift in gifts:
+        gift.wait_send()
 
 
 def on_device(q, nk, nv, ck, cv, lengths, res, wo, gain, wg, wu, wd):
     vmem = pl.BlockSpec(memory_space=pltpu.VMEM)
     hbm = pl.BlockSpec(memory_space=pl.ANY)
-    smem = pl.BlockSpec(memory_space=pltpu.SMEM)
     V = pltpu.VMEM
     return pl.pallas_call(
         kernel,
@@ -252,14 +311,20 @@
             jax.ShapeDtypeStruct((ROWS, 4 * HD), BF),
             jax.ShapeDtypeStruct((8, 2 * HD), BF),
         ),
-        in_specs=[vmem, vmem, vmem, hbm, hbm, smem, vmem, hbm, vmem, hbm, hbm, hbm],
+        in_specs=[hbm] * 12,
         out_specs=(vmem, vmem),
         scratch_shapes=[
+            V(q.shape, BF),
+            V(nk.shape, BF),
+            V(nv.shape, BF),
+            pltpu.SMEM((ROWS,), jnp.int32),
+            V(res.shape, BF),
+            V((3, 1, 2 * HD), F32),
             V((ROWS, SPAN * KV, HD), BF),
             V((ROWS, SPAN * KV, HD), BF),
             V(wo.shape, BF),
-            V(wg.shape, BF),
-            V(wu.shape, BF),
+            V((2, 2 * HD, 4 * HD), BF),
+            V((2, 2 * HD, 4 * HD), BF),
             V(wd.shape, BF),
             V((F, 16, 2 * HD), BF),
             V((F, 16, 2 * HD), BF),
@@ -268,9 +333,9 @@
             V((F, 16, HD), BF),
             V((F, 16, HD), BF),
             V((16, HD), BF),
-            V((F, 16, HD), BF),
-            V((F, 2, 64, HD), BF),
-            V((A, 64, HD), BF),
+            V((3 * F, 16, HD), BF),
+            V((F, 64, HD), BF),
+            V((F, 64, HD), BF),
             V((32, HD), BF),
             V((A, 32, HD), BF),
             V((F, 16, HD), BF),
@@ -278,10 +343,12 @@
             V((ROWS * HEADS, 2 * HD), BF),
             V((16, HD), F32),
             V((A * 16, HD), F32),
-            pltpu.SemaphoreType.DMA((2 * ROWS + 4,)),
+            pltpu.SemaphoreType.DMA((2 * ROWS + 12,)),
             pltpu.SemaphoreType.DMA((7,)),
             pltpu.SemaphoreType.DMA((7,)),
-            pltpu.SemaphoreType.DMA((A,)),
+            pltpu.SemaphoreType.DMA((F,)),
+            pltpu.SemaphoreType.DMA((6,)),
+            pltpu.SemaphoreType.DMA((6,)),
         ],
         compiler_params=pltpu.CompilerParams(
             collective_id=0, has_side_effects=True, vmem_limit_bytes=60 * 1024 * 1024

time: 69.3 us -> 63.7 us (0.919)
  Pallas kernels: 66.6 us -> 61 us
    pallas_call x1, Pallas kernels: 66.6 us -> 61 us  [on_device(): pl.pallas_call(kernel, out_shape=(jax.ShapeDtypeStruct((ROWS, 4 * HD), BF...]
where the time goes in v3:
time: 63.7 us; the launch traced here: 63.6 us
  Pallas kernels  61 us (96%)
  local copies, waits for them, and re-layouts  1.86 us (3%)
  between operations  0.65 us (1%)
    pallas_call x1, Pallas kernels, on_device(): pl.pallas_call(kernel, out_shape=(jax.ShapeDtypeStruct((ROWS, 4 * HD), BF...  61 us
    unnamed x4, local copies, waits for them, and re-layouts  1.86 us

profile of v3, /device:TPU:1, one launch (start us, length us, event | category | flops | bytes accessed | tf_op | source)
XLA Modules:
  0.0 63.6 jit_solution(15856418044286727752)
XLA Ops:
  0.6 61.0 %shard_map.131 = (bf16[4,512]{1,0:T(4,128)(2,1)}, bf16[8,256]{1,0:T(8,128)(2,1)}) custom-call(bf16[4,64,128]{2,1,0:T(8,128)(2,1)} %q_hbm.1, bf16[4,8,128]{2,1,0:T(8,128)(2,1)} %nk_hbm.1, bf16[4,8,128]{2,1,0:T(8,128)(2,1)} %nv_hbm.1, bf16[4,1024,128]{2,1,0:T(8,128)(2,1)} %bitcast.3, bf16[4,1024,128]{2,1,0:T(8,128)(2,1)} %bitcast.4, s32[4]{0:T(128)} %len_hbm.1, ...), custom_call_target="tpu_custom_call" | custom-call | tf_op jit(solution)/shard_map/pallas_call | solution.py:308
  61.7 0.0 copy-start
  61.7 1.3 %copy.16 = bf16[4,512]{1,0:T(4,128)(2,1)} copy(bf16[4,512]{1,0:T(4,128)(2,1)} %get-tuple-element.4) | data formatting | bytes 8192
  63.0 0.0 copy-done
  63.0 0.6 copy.17
Async XLA Ops:
  61.7 1.3 %copy-start = (bf16[8,256]{1,0:T(8,128)(2,1)S(1)}, bf16[8,256]{1,0:T(8,128)(2,1)}, u32[]{:S(2)}) copy-start(bf16[8,256]{1,0:T(8,128)(2,1)} %get-tuple-element.5) | copy-start | bytes 12292

commit v4 on v3

--- a/solution.py
+++ b/solution.py
@@ -31,8 +31,8 @@
 )
 COLUMN_SHIFTS = [s for s in ATTN_SHIFTS if s[0] % 2 == 0]
 BLOCK_SHIFTS = sorted(
-    ((x, z, c, w) for x in range(4) for z in range(2) for c in range(2) for w in range(3) if x or z or c or w),
-    key=lambda s: (-(min(s[0], 4 - s[0]) + s[1] + s[2] / 2 + min(s[3], 1)), s),
+    ((x, c, w) for x in range(4) for c in range(2) for w in range(3) if x or c or w),
+    key=lambda s: (-(min(s[0], 4 - s[0]) + s[1] / 2 + min(s[2], 1)), s),
 )
 
 
@@ -52,13 +52,23 @@
     return lax.dot_general(a, b, (((1,), (1,)), ((), ())), preferred_element_type=F32)
 
 
+def pair_of(f):
+    return ((f >> 2) << 1) | (f & 1)
+
+
+def in_pairs(x):
+    return jnp.stack([x[(p >> 1) * 4 + z * 2 + (p & 1)] for p in range(F // 2) for z in range(2)], axis=0).reshape(
+        (F // 2, 2) + x.shape[1:]
+    )
+
+
 def kernel(
     q_hbm, nk_hbm, nv_hbm, k_hbm, v_hbm, len_hbm, res_hbm, wo_hbm, gain_hbm, wg_hbm, wu_hbm, wd_hbm,
-    att_out, layer_out,
+    fin,
     q_ref, nk_ref, nv_ref, len_ref, res_ref, gain_ref, k_s, v_s, wo_s, wg_s, wu_s, wd_s,
     snd_a, rcv_a, msg_b, rcv_b, snd_c, rcv_c, msg_e, rcv_e, snd_f, rcv_f, msg_g, rcv_g, snd_h, rcv_h,
-    x_s, att_s, gath_s,
-    load_sem, send_sem, recv_sem, recv_f_sem, give_send, give_recv,
+    x_s, gath_s,
+    load_sem, send_sem, recv_sem, recv_f_sem, give_send, give_recv, res_sem, res_s,
 ):
     a = lax.axis_index("attn")
     f = lax.axis_index("ffn")
@@ -66,15 +76,17 @@
     gate_with = a ^ 4
     up_with = ((((a >> 2) + 2 * odd - 1) & 7) << 2) | (a & 3)
     owners = (a, gate_with, up_with)
+    level = (f >> 1) & 1
     group = ((a >> 3) << 2) | (a & 3)
 
     barrier = pltpu.get_barrier_semaphore()
+    for shift in FFN_SHIFTS:
+        pl.semaphore_signal(barrier, inc=1, device_id=(a, ffn_at(f, shift)), device_id_type=MESH)
     for shift in ATTN_SHIFTS:
         pl.semaphore_signal(barrier, inc=1, device_id=(attn_at(a, shift), f), device_id_type=MESH)
-    for shift in BLOCK_SHIFTS:
-        if shift[:3] != (0, 0, 0):
-            peer = (owners[shift[3]], ffn_at(f, shift))
-            pl.semaphore_signal(barrier, inc=1, device_id=peer, device_id_type=MESH)
+    for x, c, w in BLOCK_SHIFTS:
+        if w and (x or c):
+            pl.semaphore_signal(barrier, inc=1, device_id=(owners[w], ffn_at(f, (x, 0, c))), device_id_type=MESH)
 
     def load(src, dst, i):
         return pltpu.make_async_copy(src, dst, load_sem.at[i])
@@ -169,8 +181,15 @@
     perm = (j == ((i >> 2) & 3) * HEADS + (i >> 4) * 4 + (i & 3)).astype(F32).astype(BF)
     snd_a[...] = dot(perm, x_s[...]).astype(BF).reshape(F, 16, 2 * HD)
 
-    pl.semaphore_wait(barrier, A - 1 + 3 * (F - 1))
+    pl.semaphore_wait(barrier, A + F - 2 + 2 * (F // 2 - 1))
+    res = res_ref[...].astype(F32)
+    res_s[level] = jnp.concatenate([res[:, :HD], res[:, HD:]], axis=0).astype(BF)
     to_ffn(lambda to: snd_a.at[to], rcv_a, 0)
+    res_gift = pltpu.make_async_remote_copy(
+        src_ref=res_s.at[level], dst_ref=res_s.at[level], send_sem=res_sem.at[0], recv_sem=res_sem.at[1],
+        device_id=(a, f ^ 2), device_id_type=MESH,
+    )
+    res_gift.start()
     gifts = [
         give(wg_hbm.at[:, their_half], wg_s.at[1, :, pl.ds(0, 3 * HD)], gate_with, 0),
         give(wu_hbm.at[:, their_half], wu_s.at[1, :, pl.ds(0, 3 * HD)], up_with, 1),
@@ -195,9 +214,7 @@
     for gift in gifts:
         gift.start()
     rcv_b[a] = msg_b[...]
-    att_s[...] = msg_b[...].astype(F32)
-    for h in range(4):
-        att_out[:, h * HD : (h + 1) * HD] = att_s[pl.ds(h, ROWS, stride=4), :].astype(BF)
+    fin[:16] = msg_b[...].astype(F32)
     loads[0].wait()
     wait_all(rcv_b, A, recv_sem.at[1])
 
@@ -208,25 +225,29 @@
         x = x.reshape(F, 8, 2 * HD)
         return jnp.concatenate([x[:, :, :HD], x[:, :, HD:]], axis=1)
 
-    snd_c[...] = halves(dot(lhs, wo_s[...])).astype(BF)
-    to_ffn(lambda to: snd_c.at[to], rcv_c, 2)
-    rcv_c[f] = snd_c[f]
-    res = res_ref[...].astype(F32)
-    res = jnp.concatenate([res[:, :HD], res[:, HD:]], axis=0)
+    snd_c[...] = in_pairs(halves(dot(lhs, wo_s[...]))).astype(BF)
+    for shift in FFN_SHIFTS:
+        to = ffn_at(f, shift)
+        pltpu.make_async_remote_copy(
+            src_ref=snd_c.at[pair_of(to)], dst_ref=rcv_c.at[f], send_sem=send_sem.at[2], recv_sem=recv_sem.at[2],
+            device_id=(a, to), device_id_type=MESH,
+        ).start()
+    rcv_c[f] = snd_c[pair_of(f)]
+    res_gift.wait_recv()
     wait_all(rcv_c, F, recv_sem.at[2])
-    msg_e[...] = (res + jnp.sum(rcv_c[...].astype(F32), axis=0)).astype(BF)
-
-    for shift in BLOCK_SHIFTS:
+    msg_e[...] = (res_s[...].astype(F32) + jnp.sum(rcv_c[...].astype(F32), axis=0)).astype(BF)
+
+    for x, c, w in BLOCK_SHIFTS:
         pltpu.make_async_remote_copy(
-            src_ref=msg_e, dst_ref=rcv_e.at[shift[3] * F + f], send_sem=send_sem.at[3], recv_sem=recv_sem.at[3],
-            device_id=(owners[shift[3]], ffn_at(f, shift)), device_id_type=MESH,
+            src_ref=msg_e, dst_ref=rcv_e.at[w * (F // 2) + pair_of(f)], send_sem=send_sem.at[3], recv_sem=recv_sem.at[3],
+            device_id=(owners[w], ffn_at(f, (x, 0, c))), device_id_type=MESH,
         ).start()
-    rcv_e[f] = msg_e[...]
+    rcv_e[pair_of(f)] = msg_e[...]
     for copy in loads[2:]:
         copy.wait()
     for gift in gifts:
         gift.wait_recv()
-    wait_all(rcv_e, 3 * F, recv_sem.at[3])
+    wait_all(rcv_e, 3 * F // 2, recv_sem.at[3])
     wide = rcv_e[...].astype(F32).reshape(3, F, 16, HD)
     squares = jnp.zeros((F * 8, 1), F32)
     normed = []
@@ -284,16 +305,17 @@
     cols = [even[:, :8], even[:, 8:16], even[:, 16:24], mid, odds[:, :8], odds[:, 8:16], odds[:, 16:24]]
     hidden = jnp.concatenate([c.reshape(F * 8, HD) for c in cols], axis=1).astype(BF)
     snd_h[...] = halves(dot(hidden, wd_s[...])).astype(BF)
-    to_ffn(lambda to: snd_h.at[to], rcv_h, 6)
-    rcv_h[f] = snd_h[f]
+    to_ffn(lambda to: snd_h.at[pair_of(to) * 2 + ((to >> 1) & 1)], rcv_h, 6)
+    rcv_h[f] = snd_h[pair_of(f) * 2 + level]
     wait_all(rcv_h, F, recv_sem.at[6])
-    done = msg_e[...].astype(F32) + jnp.sum(rcv_h[...].astype(F32), axis=0)
-    layer_out[...] = jnp.concatenate([done[:8], done[8:]], axis=1).astype(BF)
+    done = msg_e[level].astype(F32) + jnp.sum(rcv_h[...].astype(F32), axis=0)
+    fin[16:] = done
 
     wait_all(rcv_a, F, send_sem.at[0])
     wait_all(rcv_b, A, send_sem.at[1])
     wait_all(rcv_c, F, send_sem.at[2])
-    wait_all(rcv_e, 3 * F, send_sem.at[3])
+    wait_all(rcv_e, 3 * F // 2, send_sem.at[3])
+    res_gift.wait_send()
     wait_all(rcv_f, F, send_sem.at[4])
     wait_all(rcv_g, A, send_sem.at[5])
     wait_all(rcv_h, F, send_sem.at[6])
@@ -301,18 +323,21 @@
         gift.wait_send()
 
 
+def finish(fin, att_out, layer_out):
+    for h in range(4):
+        att_out[:, h * HD : (h + 1) * HD] = fin[pl.ds(h, ROWS, stride=4), :].astype(BF)
+    layer_out[...] = jnp.concatenate([fin[16:24], fin[24:]], axis=1).astype(BF)
+
+
 def on_device(q, nk, nv, ck, cv, lengths, res, wo, gain, wg, wu, wd):
     vmem = pl.BlockSpec(memory_space=pltpu.VMEM)
     hbm = pl.BlockSpec(memory_space=pl.ANY)
     V = pltpu.VMEM
-    return pl.pallas_call(
+    fin = pl.pallas_call(
         kernel,
-        out_shape=(
-            jax.ShapeDtypeStruct((ROWS, 4 * HD), BF),
-            jax.ShapeDtypeStruct((8, 2 * HD), BF),
-        ),
+        out_shape=jax.ShapeDtypeStruct((32, HD), F32),
         in_specs=[hbm] * 12,
-        out_specs=(vmem, vmem),
+        out_specs=vmem,
         scratch_shapes=[
             V(q.shape, BF),
             V(nk.shape, BF),
@@ -330,10 +355,10 @@
             V((F, 16, 2 * HD), BF),
             V((16, HD), BF),
             V((A, 16, HD), BF),
-            V((F, 16, HD), BF),
-            V((F, 16, HD), BF),
-            V((16, HD), BF),
-            V((3 * F, 16, HD), BF),
+            V((F // 2, 2, 16, HD), BF),
+            V((F, 2, 16, HD), BF),
+            V((2, 16, HD), BF),
+            V((3 * F // 2, 2, 16, HD), BF),
             V((F, 64, HD), BF),
             V((F, 64, HD), BF),
             V((32, HD), BF),
@@ -341,7 +366,6 @@
             V((F, 16, HD), BF),
             V((F, 16, HD), BF),
             V((ROWS * HEADS, 2 * HD), BF),
-            V((16, HD), F32),
             V((A * 16, HD), F32),
             pltpu.SemaphoreType.DMA((2 * ROWS + 12,)),
             pltpu.SemaphoreType.DMA((7,)),
@@ -349,6 +373,8 @@
             pltpu.SemaphoreType.DMA((F,)),
             pltpu.SemaphoreType.DMA((6,)),
             pltpu.SemaphoreType.DMA((6,)),
+            pltpu.SemaphoreType.DMA((2,)),
+            V((2, 16, HD), BF),
         ],
         compiler_params=pltpu.CompilerParams(
             collective_id=0, has_side_effects=True, vmem_limit_bytes=60 * 1024 * 1024
@@ -358,6 +384,12 @@
         ck.reshape(ROWS, SPAN * KV, HD), cv.reshape(ROWS, SPAN * KV, HD),
         lengths, res, wo, gain.reshape(1, 2 * HD), wg, wu, wd,
     )
+    return pl.pallas_call(
+        finish,
+        out_shape=(jax.ShapeDtypeStruct((ROWS, 4 * HD), BF), jax.ShapeDtypeStruct((8, 2 * HD), BF)),
+        in_specs=[vmem],
+        out_specs=(vmem, vmem),
+    )(fin)
 
 
 def solution(mesh):

time: 63.7 us -> 62.9 us (0.987)
  local copies, waits for them, and re-layouts: 1.86 us -> 0 us
  Pallas kernels: 61 us -> 62 us
    unnamed x4 -> x0, local copies, waits for them, and re-layouts: 1.86 us -> none
    pallas_call x1 -> x2, Pallas kernels: 61 us -> 62 us  [the longest x1 60.7 us: on_device(): pl.pallas_call(kernel, out_shape=jax.ShapeDtypeStruct((32, HD), F32), in_...]
where the time goes in v4:
time: 62.9 us; the launch traced here: 62.7 us
  Pallas kernels  62 us (99%)
  between operations  0.64 us (1%)
    pallas_call x1, Pallas kernels, on_device(): pl.pallas_call(kernel, out_shape=jax.ShapeDtypeStruct((32, HD), F32), in_...  60.7 us
    pallas_call x1, Pallas kernels, on_device(): pl.pallas_call(finish, out_shape=(jax.ShapeDtypeStruct((ROWS, 4 * HD), BF...  1.32 us

profile of v4, /device:TPU:1, one launch (start us, length us, event | category | flops | bytes accessed | tf_op | source)
XLA Modules:
  0.0 62.7 jit_solution(11269245623953816319)
XLA Ops:
  0.6 60.7 %shard_map.131.fin = f32[32,128]{1,0:T(8,128)} custom-call(bf16[4,64,128]{2,1,0:T(8,128)(2,1)} %q_hbm.1, bf16[4,8,128]{2,1,0:T(8,128)(2,1)} %nk_hbm.1, bf16[4,8,128]{2,1,0:T(8,128)(2,1)} %nv_hbm.1, bf16[4,1024,128]{2,1,0:T(8,128)(2,1)} %bitcast.3, bf16[4,1024,128]{2,1,0:T(8,128)(2,1)} %bitcast.4, s32[4]{0:T(128)} %len_hbm.1, bf16[8,256]{1,0:T(8,128)(2,1)} %res_hbm.1, ...), custom_call_target="tpu_custom_call" | custom-call | tf_op jit(solution)/shard_map/pallas_call | solution.py:336
  61.3 1.3 %shard_map.132 = (bf16[4,512]{1,0:T(4,128)(2,1)}, bf16[8,256]{1,0:T(8,128)(2,1)}) custom-call(f32[32,128]{1,0:T(8,128)} %shard_map.131.fin), custom_call_target="tpu_custom_call" | custom-call | tf_op jit(solution)/shard_map/pallas_call | solution.py:387

commit v5 on v4

--- a/solution.py
+++ b/solution.py
@@ -34,6 +34,10 @@
     ((x, c, w) for x in range(4) for c in range(2) for w in range(3) if x or c or w),
     key=lambda s: (-(min(s[0], 4 - s[0]) + s[1] / 2 + min(s[2], 1)), s),
 )
+LAUNCH = sorted(
+    range(A),
+    key=lambda a: ((0, 0.9, 1.8, 2.6, 4.4, 4.3, 3.6, 2.9)[a >> 2] + (0, 1.8, 5.0, 6.5)[a & 3], a),
+)
 
 
 def attn_at(a, shift, sign=1):
@@ -68,7 +72,7 @@
     q_ref, nk_ref, nv_ref, len_ref, res_ref, gain_ref, k_s, v_s, wo_s, wg_s, wu_s, wd_s,
     snd_a, rcv_a, msg_b, rcv_b, snd_c, rcv_c, msg_e, rcv_e, snd_f, rcv_f, msg_g, rcv_g, snd_h, rcv_h,
     x_s, gath_s,
-    load_sem, send_sem, recv_sem, recv_f_sem, give_send, give_recv, res_sem, res_s,
+    load_sem, send_sem, recv_sem, recv_f_sem, give_send, give_recv, res_sem, res_s, near_sem, far_sem,
 ):
     a = lax.axis_index("attn")
     f = lax.axis_index("ffn")
@@ -79,14 +83,23 @@
     level = (f >> 1) & 1
     group = ((a >> 3) << 2) | (a & 3)
 
+    core = f & 1
+    sibling = (a, f ^ 1)
     barrier = pltpu.get_barrier_semaphore()
+
+    def greet(peer):
+        pl.semaphore_signal(barrier, inc=1, device_id=peer, device_id_type=MESH)
+
     for shift in FFN_SHIFTS:
-        pl.semaphore_signal(barrier, inc=1, device_id=(a, ffn_at(f, shift)), device_id_type=MESH)
+        if shift[2] == 0:
+            greet((a, ffn_at(f, shift) & ~1))
+
+    @pl.when(core == 1)
+    def _():
+        greet(sibling)
+
     for shift in ATTN_SHIFTS:
-        pl.semaphore_signal(barrier, inc=1, device_id=(attn_at(a, shift), f), device_id_type=MESH)
-    for x, c, w in BLOCK_SHIFTS:
-        if w and (x or c):
-            pl.semaphore_signal(barrier, inc=1, device_id=(owners[w], ffn_at(f, (x, 0, c))), device_id_type=MESH)
+        greet((attn_at(a, shift), f | 1))
 
     def load(src, dst, i):
         return pltpu.make_async_copy(src, dst, load_sem.at[i])
@@ -143,35 +156,58 @@
         view = buf.at[pl.ds(0, n - 1)]
         pltpu.make_async_copy(view, view, sem).wait()
 
-    col = lax.broadcasted_iota(jnp.int32, (HEADS, SPAN * KV), 1)
-    head = lax.broadcasted_iota(jnp.int32, (HEADS, SPAN * KV), 0)
-    match = (col & 7) == (head >> 3)
+    lane = lax.broadcasted_iota(jnp.int32, (KV, HD), 1)
+    col = lax.broadcasted_iota(jnp.int32, (KV, SPAN * KV), 1)
+    kind, own_kind = col & 7, lane & 7
     place = (col >> 3) + f * SPAN
-    own_ok = jnp.logical_and(
-        match[:, :HD], jnp.logical_and(col[:, :HD] < KV, jnp.full((HEADS, HD), f, jnp.int32) == 0)
-    )
-    low_lane = lax.broadcasted_iota(jnp.int32, (HEADS, HD), 1) < HD // 2
+    own_ok = jnp.logical_and(lane < KV, jnp.full((KV, HD), f, jnp.int32) == 0)
     scale = 1.0 / math.sqrt(HD)
     pad = jnp.zeros((HD - KV, HD), BF)
+    low_lane = lax.broadcasted_iota(jnp.int32, (HEADS, HD), 1) < HD // 2
+
+    def fold(x, kinds):
+        y = x[:KV]
+        for k in range(1, KV):
+            y = jnp.where(kinds == k, x[k * KV : (k + 1) * KV], y)
+        return y
+
+    def unfold(x, kinds):
+        return jnp.concatenate([jnp.where(kinds == k, x, 0.0) for k in range(KV)], axis=0)
+
+    def over_kinds(x, op):
+        for turn in (8, 16, 32, 64):
+            x = op(x, pltpu.roll(x, turn, 1))
+        return x
+
+    def spread(x):
+        return jnp.concatenate([jnp.broadcast_to(x[:, k : k + 1], (KV, HD)) for k in range(KV)], axis=0)
+
     for copy in small:
         copy.wait()
+    for k_copy, _ in caches:
+        k_copy.wait()
+    weights = []
     for r in range(ROWS):
-        q = q_ref[r]
-        caches[r][0].wait()
-        s = dot_nt(q, k_s[r]) * scale
-        s = jnp.where(jnp.logical_and(match, place < len_ref[r]), s, LOW)
-        own = dot_nt(q, jnp.concatenate([nk_ref[r], pad], axis=0)) * scale
+        s = fold(dot_nt(q_ref[r], k_s[r]), kind) * scale
+        s = jnp.where(place < len_ref[r], s, LOW)
+        own = fold(dot_nt(q_ref[r], jnp.concatenate([nk_ref[r], pad], axis=0)), own_kind) * scale
         own = jnp.where(own_ok, own, LOW)
-        m = jnp.maximum(jnp.max(s, axis=1, keepdims=True), jnp.max(own, axis=1, keepdims=True))
-        m = jnp.maximum(m, FLOOR).astype(BF).astype(F32)
-        p = jnp.exp(s - m).astype(BF)
-        own_p = jnp.exp(own - m).astype(BF)
-        total = jnp.sum(p.astype(F32), axis=1, keepdims=True) + jnp.sum(
-            own_p.astype(F32), axis=1, keepdims=True
-        )
-        caches[r][1].wait()
+        m = own
+        for t in range(KV):
+            m = jnp.maximum(m, s[:, t * HD : (t + 1) * HD])
+        m = jnp.maximum(over_kinds(m, jnp.maximum), FLOOR).astype(BF).astype(F32)
+        p = [jnp.exp(s[:, t * HD : (t + 1) * HD] - m).astype(BF).astype(F32) for t in range(KV)]
+        own_p = jnp.exp(own - m).astype(BF).astype(F32)
+        total = own_p
+        for t in range(KV):
+            total = total + p[t]
+        total = over_kinds(total, jnp.add)
+        p = unfold(jnp.concatenate(p, axis=1), kind).astype(BF)
+        weights.append((p, unfold(own_p, own_kind).astype(BF), jnp.where(low_lane, spread(m), spread(total))))
+    for _, v_copy in caches:
+        v_copy.wait()
+    for r, (p, own_p, stats) in enumerate(weights):
         o = dot(p, v_s[r]) + dot(own_p, jnp.concatenate([nv_ref[r], pad], axis=0))
-        stats = jnp.where(low_lane, jnp.broadcast_to(m, (HEADS, HD)), jnp.broadcast_to(total, (HEADS, HD)))
         x_s[pl.ds(r * HEADS, HEADS), :] = jnp.concatenate([o, stats], axis=1).astype(BF)
     for copy in loads:
         copy.start()
@@ -181,7 +217,15 @@
     perm = (j == ((i >> 2) & 3) * HEADS + (i >> 4) * 4 + (i & 3)).astype(F32).astype(BF)
     snd_a[...] = dot(perm, x_s[...]).astype(BF).reshape(F, 16, 2 * HD)
 
-    pl.semaphore_wait(barrier, A + F - 2 + 2 * (F // 2 - 1))
+    @pl.when(core == 0)
+    def _():
+        pl.semaphore_wait(barrier, F - 1)
+        pl.semaphore_signal(near_sem, inc=1, device_id=sibling, device_id_type=MESH)
+
+    @pl.when(core == 1)
+    def _():
+        pl.semaphore_wait(near_sem, 1)
+
     res = res_ref[...].astype(F32)
     res_s[level] = jnp.concatenate([res[:, :HD], res[:, HD:]], axis=0).astype(BF)
     to_ffn(lambda to: snd_a.at[to], rcv_a, 0)
@@ -199,6 +243,12 @@
         give(gain_ref.at[0], gain_ref.at[2], up_with, 5),
     ]
     rcv_a[f] = snd_a[f]
+
+    @pl.when(core == 1)
+    def _():
+        pl.semaphore_wait(barrier, 2 * (A - 1))
+        pl.semaphore_signal(far_sem, inc=1, device_id=sibling, device_id_type=MESH)
+
     wait_all(rcv_a, F, recv_sem.at[0])
 
     parts = rcv_a[...].astype(F32)
@@ -210,6 +260,11 @@
     e = jnp.exp(m - jnp.max(m, axis=0, keepdims=True))
     att = jnp.sum(parts[:, :, :HD] * e, axis=0) / jnp.sum(t * e, axis=0)
     msg_b[...] = att.astype(BF)
+
+    @pl.when(core == 0)
+    def _():
+        pl.semaphore_wait(far_sem, 1)
+
     to_attn(lambda to: msg_b, rcv_b, 1, recv_sem.at[1])
     for gift in gifts:
         gift.start()
@@ -293,7 +348,15 @@
     half = jnp.where(is_odd, pltpu.roll(hidden[24:], HD // 2, 1), hidden[24:])
     msg_g[...] = jnp.concatenate([hidden[:24], half], axis=0).astype(BF)
 
-    to_attn(lambda to: msg_g, rcv_g, 5, recv_sem.at[5])
+    for to in LAUNCH:
+
+        @pl.when(a != to)
+        def _():
+            pltpu.make_async_remote_copy(
+                src_ref=msg_g, dst_ref=rcv_g.at[a], send_sem=send_sem.at[5], recv_sem=recv_sem.at[5],
+                device_id=(to, f), device_id_type=MESH,
+            ).start()
+
     rcv_g[a] = msg_g[...]
     loads[1].wait()
     wait_all(rcv_g, A, recv_sem.at[5])
@@ -375,6 +438,8 @@
             pltpu.SemaphoreType.DMA((6,)),
             pltpu.SemaphoreType.DMA((2,)),
             V((2, 16, HD), BF),
+            pltpu.SemaphoreType.REGULAR,
+            pltpu.SemaphoreType.REGULAR,
         ],
         compiler_params=pltpu.CompilerParams(
             collective_id=0, has_side_effects=True, vmem_limit_bytes=60 * 1024 * 1024

time: 62.9 us -> 61.9 us (0.984)
  Pallas kernels: 62 us -> 61 us
    pallas_call x1, Pallas kernels: 60.7 us -> 59.7 us  [on_device(): pl.pallas_call(kernel, out_shape=jax.ShapeDtypeStruct((32, HD), F32), in_...]
where the time goes in v5:
time: 61.9 us; the launch traced here: 61.7 us
  Pallas kernels  61 us (99%)
  between operations  0.64 us (1%)
    pallas_call x1, Pallas kernels, on_device(): pl.pallas_call(kernel, out_shape=jax.ShapeDtypeStruct((32, HD), F32), in_...  59.7 us
    pallas_call x1, Pallas kernels, on_device(): pl.pallas_call(finish, out_shape=(jax.ShapeDtypeStruct((ROWS, 4 * HD), BF...  1.32 us

profile of v5, /device:TPU:1, one launch (start us, length us, event | category | flops | bytes accessed | tf_op | source)
XLA Modules:
  0.0 61.7 jit_solution(2630034647448949669)
XLA Ops:
  0.6 59.7 %shard_map.131.fin = f32[32,128]{1,0:T(8,128)} custom-call(bf16[4,64,128]{2,1,0:T(8,128)(2,1)} %q_hbm.1, bf16[4,8,128]{2,1,0:T(8,128)(2,1)} %nk_hbm.1, bf16[4,8,128]{2,1,0:T(8,128)(2,1)} %nv_hbm.1, bf16[4,1024,128]{2,1,0:T(8,128)(2,1)} %bitcast.3, bf16[4,1024,128]{2,1,0:T(8,128)(2,1)} %bitcast.4, s32[4]{0:T(128)} %len_hbm.1, bf16[8,256]{1,0:T(8,128)(2,1)} %res_hbm.1, ...), custom_call_target="tpu_custom_call" | custom-call | tf_op jit(solution)/shard_map/pallas_call | solution.py:399
  60.4 1.3 %shard_map.132 = (bf16[4,512]{1,0:T(4,128)(2,1)}, bf16[8,256]{1,0:T(8,128)(2,1)}) custom-call(f32[32,128]{1,0:T(8,128)} %shard_map.131.fin), custom_call_target="tpu_custom_call" | custom-call | tf_op jit(solution)/shard_map/pallas_call | solution.py:452

commit v6 on v5

--- a/solution.py
+++ b/solution.py
@@ -68,11 +68,11 @@
 
 def kernel(
     q_hbm, nk_hbm, nv_hbm, k_hbm, v_hbm, len_hbm, res_hbm, wo_hbm, gain_hbm, wg_hbm, wu_hbm, wd_hbm,
-    fin,
+    fin_hbm,
     q_ref, nk_ref, nv_ref, len_ref, res_ref, gain_ref, k_s, v_s, wo_s, wg_s, wu_s, wd_s,
     snd_a, rcv_a, msg_b, rcv_b, snd_c, rcv_c, msg_e, rcv_e, snd_f, rcv_f, msg_g, rcv_g, snd_h, rcv_h,
     x_s, gath_s,
-    load_sem, send_sem, recv_sem, recv_f_sem, give_send, give_recv, res_sem, res_s, near_sem, far_sem,
+    load_sem, send_sem, recv_sem, recv_f_sem, give_send, give_recv, res_sem, res_s, near_sem, far_sem, fin, fin_sem,
 ):
     a = lax.axis_index("attn")
     f = lax.axis_index("ffn")
@@ -374,6 +374,9 @@
     done = msg_e[level].astype(F32) + jnp.sum(rcv_h[...].astype(F32), axis=0)
     fin[16:] = done
 
+    result = pltpu.make_async_copy(fin, fin_hbm, fin_sem)
+    result.start()
+
     wait_all(rcv_a, F, send_sem.at[0])
     wait_all(rcv_b, A, send_sem.at[1])
     wait_all(rcv_c, F, send_sem.at[2])
@@ -384,6 +387,7 @@
     wait_all(rcv_h, F, send_sem.at[6])
     for gift in gifts:
         gift.wait_send()
+    result.wait()
 
 
 def finish(fin, att_out, layer_out):
@@ -400,7 +404,7 @@
         kernel,
         out_shape=jax.ShapeDtypeStruct((32, HD), F32),
         in_specs=[hbm] * 12,
-        out_specs=vmem,
+        out_specs=hbm,
         scratch_shapes=[
             V(q.shape, BF),
             V(nk.shape, BF),
@@ -440,6 +444,8 @@
             V((2, 16, HD), BF),
             pltpu.SemaphoreType.REGULAR,
             pltpu.SemaphoreType.REGULAR,
+            V((32, HD), F32),
+            pltpu.SemaphoreType.DMA,
         ],
         compiler_params=pltpu.CompilerParams(
             collective_id=0, has_side_effects=True, vmem_limit_bytes=60 * 1024 * 1024

time: 61.9 us -> 61.9 us (level)
  no operation moved by 1% of the time
where the time goes in v6:
time: 61.9 us; the launch traced here: 61.7 us
  Pallas kernels  61 us (99%)
  between operations  0.64 us (1%)
    pallas_call x1, Pallas kernels, on_device(): pl.pallas_call(kernel, out_shape=jax.ShapeDtypeStruct((32, HD), F32), in_...  59.7 us
    pallas_call x1, Pallas kernels, on_device(): pl.pallas_call(finish, out_shape=(jax.ShapeDtypeStruct((ROWS, 4 * HD), BF...  1.32 us

profile of v6, /device:TPU:1, one launch (start us, length us, event | category | flops | bytes accessed | tf_op | source)
XLA Modules:
  0.0 61.7 jit_solution(13710357745809563083)
XLA Ops:
  0.6 59.7 %shard_map.131.fin = f32[32,128]{1,0:T(8,128)} custom-call(bf16[4,64,128]{2,1,0:T(8,128)(2,1)} %q_hbm.1, bf16[4,8,128]{2,1,0:T(8,128)(2,1)} %nk_hbm.1, bf16[4,8,128]{2,1,0:T(8,128)(2,1)} %nv_hbm.1, bf16[4,1024,128]{2,1,0:T(8,128)(2,1)} %bitcast.3, bf16[4,1024,128]{2,1,0:T(8,128)(2,1)} %bitcast.4, s32[4]{0:T(128)} %len_hbm.1, bf16[8,256]{1,0:T(8,128)(2,1)} %res_hbm.1, ...), custom_call_target="tpu_custom_call" | custom-call | tf_op jit(solution)/shard_map/pallas_call | solution.py:403
  60.3 1.3 %shard_map.132 = (bf16[4,512]{1,0:T(4,128)(2,1)}, bf16[8,256]{1,0:T(8,128)(2,1)}) custom-call(f32[32,128]{1,0:T(8,128)} %shard_map.131.fin), custom_call_target="tpu_custom_call" | custom-call | tf_op jit(solution)/shard_map/pallas_call | solution.py:458
